TPU v7x, 32 devices: a whole 2x2x4 slice. The times are simulated.
32 devices in a mesh: groups: 2 (over y), samples: 8 (over z, x), terms: 2 (over core).
Axes of the slice: x: 2, y: 2, z: 4, core: 2. Of those that a mesh axis runs over, the one named last changes fastest.
Arguments:
- sample_points: float32 [8192, 10], P(('groups', 'samples')), parts along dimension 0, may hold values from -1 to 1
- observed: float32 [8192, 48], P(('groups', 'samples')), parts along dimension 0, may hold values from -60 to 60
- multi_index: int32 [8008, 10], replicated, may hold values from 0 to 6, as said below
Outputs:
- coefficients: float32 [16016, 48], P(('groups', 'terms')), parts along dimension 0
- left_vectors: float32 [8192, 48], P(('groups', 'samples')), parts along dimension 0
There are 2 independent parts, one for each index of `groups`. A program takes and returns all parts, laid end to end along the dimension named above; an argument that names none is the same for every part. Nothing has to cross between parts.
Inputs may be any that keep to these rules, and one draw needn't show every extreme that they name: `multi_index`: each row holds the degrees of the 10 inputs in one basis term; the rows are all multi-indices of total degree at most 6, each once, in some order.
All inputs are finite; a program needn't handle non-finite values.
Results may differ from a plain program's by a relative error of at most 0.0052.
Values sent between devices are 32-bit elements; how exact they have to be, the bound alone decides.
A program may use at most 64 MiB of HBM per device.

v0:
```python
import math

import jax
import jax.numpy as jnp
from jax import lax
from jax.sharding import PartitionSpec as P

DEGREE = 6
TERMS = 8008
ITERS = 2


EPS = 1e-06


def legendre(points):
    values = [jnp.ones_like(points), points]
    for order in range(1, DEGREE):
        values.append(
            ((2 * order + 1) * points * values[order] - order * values[order - 1]) / (order + 1)
        )
    values = values[: DEGREE + 1]
    factors = jnp.sqrt(jnp.arange(DEGREE + 1, dtype=jnp.float32) * 2 + 1)
    return jnp.stack(values, axis=-1) * factors


def pair_values(points):
    values = legendre(points)
    code_width = (DEGREE + 1) ** 2
    joined = values[:, 0::2, :, None] * values[:, 1::2, None, :]
    return joined.reshape(points.shape[0], points.shape[1] // 2, code_width)


def transposed(design, left_rows):
    flipped = jnp.dot(left_rows.T, design, preferred_element_type=jnp.float32)
    return flipped.T


def build(points, table):
    term_count = table.shape[0]
    pair_count = table.shape[1] // 2
    row_count = points.shape[0]
    block_rows = math.gcd(row_count, 128)
    code_width = (DEGREE + 1) ** 2
    slots = jnp.arange(code_width, dtype=jnp.int32)[:, None]
    selectors = []
    for pair_index in range(pair_count):
        codes = table[:, 2 * pair_index] * (DEGREE + 1) + table[:, 2 * pair_index + 1]
        selectors.append((codes[None, :] == slots).astype(jnp.float32))

    def one_block(block_points):
        pair_table = pair_values(block_points)
        product = jnp.ones((block_rows, term_count), jnp.float32)
        for pair_index in range(pair_count):
            picked = jnp.dot(
                pair_table[:, pair_index, :],
                selectors[pair_index],
                precision=lax.Precision.HIGHEST,
                preferred_element_type=jnp.float32,
            )
            product = product * picked
        return (product.astype(jnp.bfloat16), jnp.sum(product * product, axis=1))

    designs, squares = lax.map(
        one_block, points.reshape(row_count // block_rows, block_rows, points.shape[1])
    )
    return (designs.reshape(row_count, term_count), squares.reshape(row_count))


def solve(row_scale, rhs, row_product, term_product, row_total, term_total, term_count):
    beta_now = jnp.sqrt(row_total(jnp.sum(rhs * rhs, axis=0)) + EPS)
    left_vec = rhs / beta_now
    raw = term_product(row_scale[:, None] * rhs) / beta_now
    alpha_now = jnp.sqrt(term_total(jnp.sum(raw * raw, axis=0)) + EPS)
    right_vec = raw / alpha_now
    direction = right_vec
    coeffs = jnp.zeros((term_count, rhs.shape[1]), jnp.float32)
    phibar = beta_now
    rhobar = alpha_now
    for iteration in range(ITERS):
        partial_value = row_scale[:, None] * row_product(right_vec) - alpha_now * left_vec
        beta_now = jnp.sqrt(row_total(jnp.sum(partial_value * partial_value, axis=0)) + EPS)
        left_vec = partial_value / beta_now
        raw = term_product(row_scale[:, None] * partial_value) / beta_now - beta_now * right_vec
        alpha_now = jnp.sqrt(term_total(jnp.sum(raw * raw, axis=0)) + EPS)
        right_vec = raw / alpha_now
        rho_val = jnp.sqrt(rhobar * rhobar + beta_now * beta_now)
        cosine = rhobar / rho_val
        sine = beta_now / rho_val
        theta_val = sine * alpha_now
        rhobar = -cosine * alpha_now
        phi_val = cosine * phibar
        phibar = sine * phibar
        coeffs = coeffs + phi_val / rho_val * direction
        direction = right_vec - theta_val / rho_val * direction
    return (coeffs, left_vec)


def per_device(sample_points, observed, multi_index):
    term_devices = lax.axis_size("terms")
    position = lax.axis_index("terms")
    total_samples = sample_points.shape[0] * lax.axis_size("samples")
    inverse_root = 1.0 / math.sqrt(total_samples)
    share = TERMS // term_devices
    my_terms = lax.dynamic_slice_in_dim(multi_index, position * share, share, 0)
    design, squares = build(sample_points, my_terms)
    squares = lax.psum(squares, "terms")
    weights = jnp.sqrt(TERMS / squares)
    row_scale = weights * inverse_root
    rhs = weights[:, None] * observed

    def row_product(right_vec):
        return lax.psum(
            jnp.dot(design, right_vec.astype(jnp.bfloat16), preferred_element_type=jnp.float32),
            "terms",
        )

    def term_product(left_rows):
        return lax.psum(transposed(design, left_rows.astype(jnp.bfloat16)), "samples")

    def row_total(column_sums):
        return lax.psum(column_sums, "samples")

    def term_total(column_sums):
        return lax.psum(column_sums, "terms")

    coeffs, left_vec = solve(
        row_scale, rhs, row_product, term_product, row_total, term_total, share
    )
    return (coeffs, left_vec)


def solution(mesh):
    in_specs = (P(("groups", "samples"), None), P(("groups", "samples"), None), P())
    out_specs = (P(("groups", "terms"), None), P(("groups", "samples"), None))
    return jax.shard_map(
        per_device, mesh=mesh, in_specs=in_specs, out_specs=out_specs, check_vma=False
    )
```

profile of v0, /device:TPU:0, one launch (start us, length us, event | category | flops | bytes accessed | tf_op | source)
XLA Modules:
  0.0 339.9 jit_solution(17378771103499737677)
XLA Ops:
  7.2 0.0 all-reduce.5.cloned.1.call-start
  7.2 0.8 reshape.330
  8.0 2.1 dynamic-slice_add_fusion
  10.1 76.3 %while.15 = (s32[]{:T(128)}, bf16[4,128,4004]{1,2,0:T(8,128)(2,1)}, f32[4,128]{1,0:T(4,128)S(1)}, f32[4,128,10]{1,0,2:T(4,128)S(1)}, s32[4004]{0:T(1024)S(1)}, /...) while((s32[]{:T(128)}, bf16[4,128,4004]{1,2,0:T(8,128)(2,1)}, ...), condition=%wide.region_2.3_spmd.clone, body=%wide.region_0.2_spmd.clone.sunk | while | flops 1512413312 | bytes 22455992 | solution.py:64
  10.2 0.1 stack.20
  10.3 0.1 broadcast_multiply_fusion.12
  10.4 3.4 %fusion.52 = f32[128,4004]{0,1:T(8,128)S(1)} fusion(s32[4004]{0:T(1024)S(1)} %get-tuple-element.306, f32[128,5,49]{0,2,1:T(8,128)S(1)} %mul.858), kind=kOutput, calls=%fused_computation.19.clone.1 | convolution fusion | flops 301749440 | bytes 2095104 | tf_op jit(solution)/shard_map/while/body/eval_jaxpr/dot_general | solution.py:55
  13.8 3.4 %convolution_multiply_fusion.7 = f32[128,4004]{0,1:T(8,128)S(1)} fusion(f32[128,4004]{0,1:T(8,128)S(1)} %fusion.52, s32[4004]{0:T(1024)S(1)} %get-tuple-element.307, f32[128,5,49]{0,2,1:T(8,128)S(1)} %mul.858), kind=kOutput, calls=%fused_computation.8.clone.1 | convolution fusion | flops 302261952 | bytes 4147200 | tf_op jit(solution)/shard_map/while/body/eval_jaxpr/dot_general | solution.py:55
  17.3 3.4 %convolution_multiply_fusion.8 = f32[128,4004]{0,1:T(8,128)S(1)} fusion(f32[128,4004]{0,1:T(8,128)S(1)} %convolution_multiply_fusion.7, s32[4004]{0:T(1024)S(1)} %get-tuple-element.308, f32[128,5,49]{0,2,1:T(8,128)S(1)} %mul.858), kind=kOutput, calls=%fused_computation.7.clone.1 | convolution fusion | flops 302261952 | bytes 4147200 | tf_op jit(solution)/shard_map/while/body/eval_jaxpr/dot_general | solution.py:55
  20.7 3.4 %convolution_multiply_fusion.9 = f32[128,4004]{0,1:T(8,128)S(1)} fusion(f32[128,4004]{0,1:T(8,128)S(1)} %convolution_multiply_fusion.8, s32[4004]{0:T(1024)S(1)} %get-tuple-element.309, f32[128,5,49]{0,2,1:T(8,128)S(1)} %mul.858), kind=kOutput, calls=%fused_computation.6.clone.1 | convolution fusion | flops 302261952 | bytes 4147200 | tf_op jit(solution)/shard_map/while/body/eval_jaxpr/dot_general | solution.py:55
  24.1 4.4 %bitcast_dynamic-update-slice_fusion.2 = (bf16[4,128,4004]{1,2,0:T(8,128)(2,1)}, f32[128,4004]{0,1:T(8,128)S(1)}) fusion(bf16[4,128,4004]{1,2,0:T(8,128)(2,1)} %get-tuple-element.291, s32[]{:T(128)} %get-tuple-element.290, f32[128,4004]{0,1:T(8,128)S(1)} %convolution_multiply_fusion.9, s32[4004]{0:T(1024)S(1)} %get-tuple-element.310, ...), kind=kOutput, calls=%fused_computation.10.clone.1 | convolution fusion | flops 302774464 | bytes 5173760 | tf_op jit(solution)/shard_map/while/body/eval_jaxpr/dot_general | solution.py:55
  28.5 0.5 multiply_reduce_fusion.7
  29.2 0.1 stack.20
  29.3 0.1 broadcast_multiply_fusion.12
  29.4 3.4 %fusion.52 = f32[128,4004]{0,1:T(8,128)S(1)} fusion(s32[4004]{0:T(1024)S(1)} %get-tuple-element.306, f32[128,5,49]{0,2,1:T(8,128)S(1)} %mul.858), kind=kOutput, calls=%fused_computation.19.clone.1 | convolution fusion | flops 301749440 | bytes 2095104 | tf_op jit(solution)/shard_map/while/body/eval_jaxpr/dot_general | solution.py:55
  32.9 3.4 %convolution_multiply_fusion.7 = f32[128,4004]{0,1:T(8,128)S(1)} fusion(f32[128,4004]{0,1:T(8,128)S(1)} %fusion.52, s32[4004]{0:T(1024)S(1)} %get-tuple-element.307, f32[128,5,49]{0,2,1:T(8,128)S(1)} %mul.858), kind=kOutput, calls=%fused_computation.8.clone.1 | convolution fusion | flops 302261952 | bytes 4147200 | tf_op jit(solution)/shard_map/while/body/eval_jaxpr/dot_general | solution.py:55
  36.3 3.4 %convolution_multiply_fusion.8 = f32[128,4004]{0,1:T(8,128)S(1)} fusion(f32[128,4004]{0,1:T(8,128)S(1)} %convolution_multiply_fusion.7, s32[4004]{0:T(1024)S(1)} %get-tuple-element.308, f32[128,5,49]{0,2,1:T(8,128)S(1)} %mul.858), kind=kOutput, calls=%fused_computation.7.clone.1 | convolution fusion | flops 302261952 | bytes 4147200 | tf_op jit(solution)/shard_map/while/body/eval_jaxpr/dot_general | solution.py:55
  39.7 3.4 %convolution_multiply_fusion.9 = f32[128,4004]{0,1:T(8,128)S(1)} fusion(f32[128,4004]{0,1:T(8,128)S(1)} %convolution_multiply_fusion.8, s32[4004]{0:T(1024)S(1)} %get-tuple-element.309, f32[128,5,49]{0,2,1:T(8,128)S(1)} %mul.858), kind=kOutput, calls=%fused_computation.6.clone.1 | convolution fusion | flops 302261952 | bytes 4147200 | tf_op jit(solution)/shard_map/while/body/eval_jaxpr/dot_general | solution.py:55
  43.1 4.4 %bitcast_dynamic-update-slice_fusion.2 = (bf16[4,128,4004]{1,2,0:T(8,128)(2,1)}, f32[128,4004]{0,1:T(8,128)S(1)}) fusion(bf16[4,128,4004]{1,2,0:T(8,128)(2,1)} %get-tuple-element.291, s32[]{:T(128)} %get-tuple-element.290, f32[128,4004]{0,1:T(8,128)S(1)} %convolution_multiply_fusion.9, s32[4004]{0:T(1024)S(1)} %get-tuple-element.310, ...), kind=kOutput, calls=%fused_computation.10.clone.1 | convolution fusion | flops 302774464 | bytes 5173760 | tf_op jit(solution)/shard_map/while/body/eval_jaxpr/dot_general | solution.py:55
  47.6 0.5 multiply_reduce_fusion.7
  48.3 0.1 stack.20
  48.3 0.1 broadcast_multiply_fusion.12
  48.5 3.4 %fusion.52 = f32[128,4004]{0,1:T(8,128)S(1)} fusion(s32[4004]{0:T(1024)S(1)} %get-tuple-element.306, f32[128,5,49]{0,2,1:T(8,128)S(1)} %mul.858), kind=kOutput, calls=%fused_computation.19.clone.1 | convolution fusion | flops 301749440 | bytes 2095104 | tf_op jit(solution)/shard_map/while/body/eval_jaxpr/dot_general | solution.py:55
  51.9 3.4 %convolution_multiply_fusion.7 = f32[128,4004]{0,1:T(8,128)S(1)} fusion(f32[128,4004]{0,1:T(8,128)S(1)} %fusion.52, s32[4004]{0:T(1024)S(1)} %get-tuple-element.307, f32[128,5,49]{0,2,1:T(8,128)S(1)} %mul.858), kind=kOutput, calls=%fused_computation.8.clone.1 | convolution fusion | flops 302261952 | bytes 4147200 | tf_op jit(solution)/shard_map/while/body/eval_jaxpr/dot_general | solution.py:55
  55.3 3.4 %convolution_multiply_fusion.8 = f32[128,4004]{0,1:T(8,128)S(1)} fusion(f32[128,4004]{0,1:T(8,128)S(1)} %convolution_multiply_fusion.7, s32[4004]{0:T(1024)S(1)} %get-tuple-element.308, f32[128,5,49]{0,2,1:T(8,128)S(1)} %mul.858), kind=kOutput, calls=%fused_computation.7.clone.1 | convolution fusion | flops 302261952 | bytes 4147200 | tf_op jit(solution)/shard_map/while/body/eval_jaxpr/dot_general | solution.py:55
  58.8 3.4 %convolution_multiply_fusion.9 = f32[128,4004]{0,1:T(8,128)S(1)} fusion(f32[128,4004]{0,1:T(8,128)S(1)} %convolution_multiply_fusion.8, s32[4004]{0:T(1024)S(1)} %get-tuple-element.309, f32[128,5,49]{0,2,1:T(8,128)S(1)} %mul.858), kind=kOutput, calls=%fused_computation.6.clone.1 | convolution fusion | flops 302261952 | bytes 4147200 | tf_op jit(solution)/shard_map/while/body/eval_jaxpr/dot_general | solution.py:55
  62.2 4.4 %bitcast_dynamic-update-slice_fusion.2 = (bf16[4,128,4004]{1,2,0:T(8,128)(2,1)}, f32[128,4004]{0,1:T(8,128)S(1)}) fusion(bf16[4,128,4004]{1,2,0:T(8,128)(2,1)} %get-tuple-element.291, s32[]{:T(128)} %get-tuple-element.290, f32[128,4004]{0,1:T(8,128)S(1)} %convolution_multiply_fusion.9, s32[4004]{0:T(1024)S(1)} %get-tuple-element.310, ...), kind=kOutput, calls=%fused_computation.10.clone.1 | convolution fusion | flops 302774464 | bytes 5173760 | tf_op jit(solution)/shard_map/while/body/eval_jaxpr/dot_general | solution.py:55
  66.6 0.5 multiply_reduce_fusion.7
  67.3 0.1 stack.20
  67.4 0.1 broadcast_multiply_fusion.12
  67.5 3.4 %fusion.52 = f32[128,4004]{0,1:T(8,128)S(1)} fusion(s32[4004]{0:T(1024)S(1)} %get-tuple-element.306, f32[128,5,49]{0,2,1:T(8,128)S(1)} %mul.858), kind=kOutput, calls=%fused_computation.19.clone.1 | convolution fusion | flops 301749440 | bytes 2095104 | tf_op jit(solution)/shard_map/while/body/eval_jaxpr/dot_general | solution.py:55
  70.9 3.4 %convolution_multiply_fusion.7 = f32[128,4004]{0,1:T(8,128)S(1)} fusion(f32[128,4004]{0,1:T(8,128)S(1)} %fusion.52, s32[4004]{0:T(1024)S(1)} %get-tuple-element.307, f32[128,5,49]{0,2,1:T(8,128)S(1)} %mul.858), kind=kOutput, calls=%fused_computation.8.clone.1 | convolution fusion | flops 302261952 | bytes 4147200 | tf_op jit(solution)/shard_map/while/body/eval_jaxpr/dot_general | solution.py:55
  74.3 3.4 %convolution_multiply_fusion.8 = f32[128,4004]{0,1:T(8,128)S(1)} fusion(f32[128,4004]{0,1:T(8,128)S(1)} %convolution_multiply_fusion.7, s32[4004]{0:T(1024)S(1)} %get-tuple-element.308, f32[128,5,49]{0,2,1:T(8,128)S(1)} %mul.858), kind=kOutput, calls=%fused_computation.7.clone.1 | convolution fusion | flops 302261952 | bytes 4147200 | tf_op jit(solution)/shard_map/while/body/eval_jaxpr/dot_general | solution.py:55
  77.8 3.4 %convolution_multiply_fusion.9 = f32[128,4004]{0,1:T(8,128)S(1)} fusion(f32[128,4004]{0,1:T(8,128)S(1)} %convolution_multiply_fusion.8, s32[4004]{0:T(1024)S(1)} %get-tuple-element.309, f32[128,5,49]{0,2,1:T(8,128)S(1)} %mul.858), kind=kOutput, calls=%fused_computation.6.clone.1 | convolution fusion | flops 302261952 | bytes 4147200 | tf_op jit(solution)/shard_map/while/body/eval_jaxpr/dot_general | solution.py:55
  81.2 4.4 %bitcast_dynamic-update-slice_fusion.2 = (bf16[4,128,4004]{1,2,0:T(8,128)(2,1)}, f32[128,4004]{0,1:T(8,128)S(1)}) fusion(bf16[4,128,4004]{1,2,0:T(8,128)(2,1)} %get-tuple-element.291, s32[]{:T(128)} %get-tuple-element.290, f32[128,4004]{0,1:T(8,128)S(1)} %convolution_multiply_fusion.9, s32[4004]{0:T(1024)S(1)} %get-tuple-element.310, ...), kind=kOutput, calls=%fused_computation.10.clone.1 | convolution fusion | flops 302774464 | bytes 5173760 | tf_op jit(solution)/shard_map/while/body/eval_jaxpr/dot_general | solution.py:55
  85.6 0.5 multiply_reduce_fusion.7
  86.4 2.8 psum.70
  89.1 6.4 %copy.17 = bf16[4,128,4004]{2,1,0:T(8,128)(2,1)} copy(bf16[4,128,4004]{1,2,0:T(8,128)(2,1)} %get-tuple-element.119) | data formatting | bytes 8200192 | tf_op jit(solution)/shard_map/while | solution.py:64
  95.5 3.9 %fusion.26 = f32[4004,48]{0,1:T(8,128)} fusion(bf16[512,4004]{1,0:T(8,128)(2,1)} %bitcast.52, f32[512,48]{0,1:T(8,128)S(1)} %copy-done.1, f32[512]{0:T(512)S(1)} %get-tuple-element.185, f32[512]{0:T(512)S(1)} %get-tuple-element.184), kind=kOutput, calls=%fused_computation.62 | convolution fusion | flops 196878336 | bytes 4971264 | tf_op jit(solution)/shard_map/dot_general | solution.py:35
  99.4 0.0 all-reduce.5.cloned.1.call-update
  99.5 0.0 all-reduce.7.cloned.1.call-start
  99.5 0.1 multiply_reduce_fusion.5
  99.6 23.2 %psum.72 = f32[48]{0:T(128)S(1)} all-reduce(f32[48]{0:T(128)S(1)} %multiply_reduce_fusion.5), channel_id=1, replica_groups=mesh['groups'=2,'samples'=8,'terms'=2] {'samples'}, use_global_device_ids=true, to_apply=%region_6.7 | all-reduce | flops 48 | bytes 384 | tf_op jit(solution)/shard_map/psum | solution.py:122
  122.8 54.0 %all-reduce.5.cloned.1.call-done = f32[4004,48]{0,1:T(8,128)} async-done(((f32[4004,48]{0,1:T(8,128)}), f32[4004,48]{0,1:T(8,128)}) %all-reduce.5.cloned.1.call-update) | async-done | bytes 768784 | tf_op jit(solution)/shard_map/psum | solution.py:119
  176.9 1.4 multiply_reduce_fusion.2
  178.2 2.5 psum.73
  180.7 4.4 %fusion.24 = f32[512,48]{0,1:T(8,128)} fusion(bf16[512,4004]{1,0:T(8,128)(2,1)} %bitcast.53, f32[4004,48]{0,1:T(8,128)} %all-reduce.5.cloned.1.call-done, f32[48]{0:T(128)S(1)} %get-tuple-element.199), kind=kOutput, calls=%fused_computation.52 | convolution fusion | flops 197188992 | bytes 4967360 | tf_op jit(solution)/shard_map/dot_general | solution.py:114
  185.1 0.0 all-reduce.7.cloned.1.call-update
  185.2 0.0 all-reduce.9.cloned.1.call-start
  185.2 17.1 %all-reduce.7.cloned.1.call-done = f32[512,48]{0,1:T(8,128)} async-done(((f32[512,48]{0,1:T(8,128)}), f32[512,48]{0,1:T(8,128)}) %all-reduce.7.cloned.1.call-update) | async-done | bytes 98320 | tf_op jit(solution)/shard_map/psum | solution.py:113
  202.3 1.1 multiply_reduce_fusion.4
  203.4 3.9 %fusion.27 = f32[4004,48]{0,1:T(8,128)} fusion(bf16[512,4004]{1,0:T(8,128)(2,1)} %bitcast.54, f32[512,48]{0,1:T(8,128)S(1)} %get-tuple-element.183, f32[512]{0:T(512)S(1)} %get-tuple-element.184), kind=kOutput, calls=%fused_computation.63 | convolution fusion | flops 196853760 | bytes 4969216 | tf_op jit(solution)/shard_map/dot_general | solution.py:35
  207.3 0.0 all-reduce.9.cloned.1.call-update
  207.3 0.0 all-reduce.11.cloned.1.call-start
  207.4 21.9 %psum.75 = f32[48]{0:T(128)S(1)} all-reduce(f32[48]{0:T(128)S(1)} %get-tuple-element.182), channel_id=1, replica_groups=mesh['groups'=2,'samples'=8,'terms'=2] {'samples'}, use_global_device_ids=true, to_apply=%region_11.12 | all-reduce | flops 48 | bytes 384 | tf_op jit(solution)/shard_map/psum | solution.py:122
  229.3 54.1 %all-reduce.9.cloned.1.call-done = f32[4004,48]{0,1:T(8,128)} async-done(((f32[4004,48]{0,1:T(8,128)}), f32[4004,48]{0,1:T(8,128)}) %all-reduce.9.cloned.1.call-update) | async-done | bytes 768784 | tf_op jit(solution)/shard_map/psum | solution.py:119
  283.5 1.5 multiply_reduce_fusion.1
  285.0 2.5 psum.77
  287.4 4.2 %fusion.22 = f32[512,48]{0,1:T(8,128)} fusion(bf16[512,4004]{1,0:T(8,128)(2,1)} %bitcast.55, f32[4004,48]{0,1:T(8,128)S(1)} %get-tuple-element.181, f32[48]{0:T(128)S(1)} %add_sqrt_fusion.2), kind=kOutput, calls=%fused_computation.49 | convolution fusion | flops 197188992 | bytes 4967360 | tf_op jit(solution)/shard_map/dot_general | solution.py:114
  291.7 17.1 %all-reduce.11.cloned.1.call-done = f32[512,48]{0,1:T(8,128)} async-done(((f32[512,48]{0,1:T(8,128)}), f32[512,48]{0,1:T(8,128)}) %all-reduce.11.cloned.1.call-update) | async-done | bytes 98320 | tf_op jit(solution)/shard_map/psum | solution.py:113
  308.8 1.1 multiply_reduce_fusion.3
  309.9 21.6 %psum.79 = f32[48]{0:T(128)S(1)} all-reduce(f32[48]{0:T(128)S(1)} %get-tuple-element.178), channel_id=1, replica_groups=mesh['groups'=2,'samples'=8,'terms'=2] {'samples'}, use_global_device_ids=true, to_apply=%region_17.18 | all-reduce | flops 48 | bytes 384 | tf_op jit(solution)/shard_map/psum | solution.py:122
  331.5 0.7 broadcast_divide_fusion.3
  332.3 1.1 multiply_add_fusion
  (50 shorter events, 0.7 us)
Async XLA Ops:
  7.2 169.7 %all-reduce.5.cloned.1.call-start = ((), (), s32[]{:S(2)}) async-start(), calls=%async_computation | async-start | bytes 1572864 | tf_op jit(solution)/shard_map/psum | solution.py:119
  89.1 6.4 %copy-start.1 = (f32[512,48]{0,1:T(8,128)S(1)}, f32[512,48]{0,1:T(8,128)}, u32[]{:S(2)}) copy-start(f32[512,48]{0,1:T(8,128)} %param.6) | copy-start | bytes 294916
  99.5 102.8 %all-reduce.7.cloned.1.call-start = ((), (), s32[]{:S(2)}) async-start(), calls=%async_computation.1 | async-start | bytes 196608 | tf_op jit(solution)/shard_map/psum | solution.py:113
  185.1 98.3 %copy-start = (f32[4004,48]{0,1:T(8,128)S(1)}, f32[4004,48]{0,1:T(8,128)}, u32[]{:S(2)}) copy-start(f32[4004,48]{0,1:T(8,128)} %all-reduce.5.cloned.1.call-done) | copy-start | bytes 2306308
  185.2 98.3 %all-reduce.9.cloned.1.call-start = ((), (), s32[]{:S(2)}) async-start(), calls=%async_computation.2 | async-start | bytes 1572864 | tf_op jit(solution)/shard_map/psum | solution.py:119
  207.3 101.5 %all-reduce.11.cloned.1.call-start = ((), (), s32[]{:S(2)}) async-start(), calls=%async_computation.3 | async-start | bytes 196608 | tf_op jit(solution)/shard_map/psum | solution.py:113
Sparse Core Ops, SparseCore 0:
  99.6 77.2 all-reduce.4
  185.3 16.9 all-reduce.6
  207.4 76.0 all-reduce.8
  291.8 16.9 all-reduce.10
where the time goes:
time: 341 us; the launch traced here: 340 us
  waiting for transfers between devices  142 us (42%)
  matrix products  88.9 us (26%)
  blocking collectives  74.4 us (22%)
  between operations  13.8 us (4%)
  other arithmetic  12 us (4%)
  local copies, waits for them, and re-layouts  7.68 us (2%)
    psum x2, waiting for transfers between devices, term_product(): lax.psum(transposed(design, left_rows.astype(jnp.bfloat16)), 'samples')  108 us
    dot_general x20, matrix products, one_block(): jnp.dot(pair_table[:, pair_index, :], selectors[pair_index], precision=la...  72.4 us
    psum x3, blocking collectives, row_total(): return lax.psum(column_sums, 'samples')  66.7 us
    psum x2, waiting for transfers between devices, row_product(): lax.psum(jnp.dot(design, right_vec.astype(jnp.bfloat16), preferred_elemen...  34.2 us
    dot_general x2, matrix products, row_product(): jnp.dot(design, right_vec.astype(jnp.bfloat16), preferred_element_type=jn...  8.64 us
    dot_general x2, matrix products, transposed(): flipped = jnp.dot(left_rows.T, design, preferred_element_type=jnp.float32)  7.81 us
  transfers between devices with their start and end apart: 4, of which 4 were waited for; matrix products, arithmetic and copies ran while one was open for 0% of the time, Pallas kernels for 0%

commit v1 on v0

v1 whole, which is shorter than its diff:
```python
import functools
import itertools
import math

import jax
import jax.numpy as jnp
import numpy as np
from jax import lax
from jax.experimental import pallas as pl
from jax.experimental.pallas import tpu as pltpu
from jax.sharding import PartitionSpec as P

INPUTS = 10
DEGREE = 6
TERMS = 8008
FIELDS = 48
EPS = 1e-06
MESH = pl.DeviceIdType.MESH

GROUPS = (((0, 1, 2), 256), ((3, 4, 5), 256), ((6, 7), 128), ((8, 9), 128))
PAD_INPUTS = 16
PIECES = 3


def group_codes(count):
    return [c for c in itertools.product(range(DEGREE + 1), repeat=count) if sum(c) <= DEGREE]


def code_key(code):
    return sum(int(d) * (DEGREE + 1) ** i for i, d in enumerate(code))


def constants():
    depth = (DEGREE + 1) * PIECES * PAD_INPUTS
    blocks = []
    keys = np.full((8, 256), -2, np.int32)
    for g, (inputs, width) in enumerate(GROUPS):
        codes = group_codes(len(inputs)) * PIECES
        for r, code in enumerate(codes):
            keys[g, r] = code_key(code)
        for i, source in enumerate(inputs):
            block = np.zeros((width, depth), np.float32)
            for r, code in enumerate(codes):
                for piece in range(PIECES):
                    block[r, (code[i] * PIECES + piece) * PAD_INPUTS + source] = 1.0
            blocks.append(block)
    return np.concatenate(blocks), keys


def pieces_of(value):
    high = value.astype(jnp.bfloat16).astype(jnp.float32)
    rest = value - high
    middle = rest.astype(jnp.bfloat16).astype(jnp.float32)
    return high, middle, rest - middle


def fit_kernel(
    n, width, share, inverse_root,
    points_ref, observed_ref, keys_ref, picks_ref, entries_ref,
    coeffs_ref, left_ref,
    design, t0, t1, t2, t3, send1, recv1, all1, send2, recv2, all2, cross_out, cross_in, norm_out, norm_in, total_in,
    rs_send, rs_recv, ag_send, ag_recv, cross_send, cross_recv, norm_send, norm_recv, tot_send, tot_recv,
):
    me = lax.axis_index("samples")
    core = lax.axis_index("terms")
    rows = points_ref.shape[1]
    tables = (t0, t1, t2, t3)

    barrier = pltpu.get_barrier_semaphore()

    def greet(step, _):
        pl.semaphore_signal(barrier, inc=1, device_id={"samples": lax.rem(me + step, n)}, device_id_type=MESH)
        return 0

    lax.fori_loop(1, n, greet, 0)
    pl.semaphore_signal(barrier, inc=1, device_id={"terms": 1 - core}, device_id_type=MESH)
    pl.semaphore_wait(barrier, n)

    x = points_ref[...]
    values = [jnp.ones_like(x), x]
    for order in range(1, DEGREE):
        values.append(
            ((2 * order + 1) * x * values[order] - order * values[order - 1]) / (order + 1)
        )
    values = [v * np.float32(math.sqrt(2 * k + 1)) for k, v in enumerate(values)]
    parts = []
    for v in values:
        parts.extend(p.astype(jnp.bfloat16) for p in pieces_of(v))
    flat = jnp.concatenate(parts, axis=0)

    offset = 0
    for g, (inputs, table_width) in enumerate(GROUPS):
        table = None
        for _ in inputs:
            factor = jnp.dot(
                picks_ref[offset:offset + table_width, :], flat, preferred_element_type=jnp.float32
            )
            table = factor if table is None else table * factor
            offset += table_width
        count = len(group_codes(len(inputs)))
        row = lax.broadcasted_iota(jnp.int32, table.shape, 0)
        high, middle, low = pieces_of(table)
        tables[g][...] = jnp.where(
            row < count, high, jnp.where(row < 2 * count, middle, low)
        ).astype(jnp.bfloat16)

    squared = [v * v for v in values]
    poly = [squared[k][0:1, :] for k in range(DEGREE + 1)]
    for j in range(1, INPUTS):
        own = [squared[k][j:j + 1, :] for k in range(DEGREE + 1)]
        fresh = []
        for d in range(DEGREE + 1):
            total = poly[d] * own[0]
            for k in range(1, d + 1):
                total = total + poly[d - k] * own[k]
            fresh.append(total)
        poly = fresh
    squares = functools.reduce(lambda a, b: a + b, poly)
    weights = jnp.sqrt(TERMS / squares)
    row_scale = weights * np.float32(inverse_root)
    rhs = weights * observed_ref[...]

    lane = lax.broadcasted_iota(jnp.int32, (FIELDS, width), 1)
    last = lane == width - 1

    def row_sums(value):
        return jnp.sum(value * value, axis=1, keepdims=True)

    def remote(src, dst, send_sem, recv_sem, peer):
        return pltpu.make_async_remote_copy(
            src_ref=src, dst_ref=dst, send_sem=send_sem, recv_sem=recv_sem,
            device_id=peer, device_id_type=MESH,
        )

    tile = min(width, 256)

    def build_chunk(q):
        def build_tile(i, _):
            at = pl.multiple_of(q * width + i * tile, tile)
            keys = keys_ref[pl.ds(at, tile), :]
            product = None
            for g, (_, table_width) in enumerate(GROUPS):
                hot = jnp.where(
                    keys[:, g:g + 1] == entries_ref[g:g + 1, 0:table_width], 1.0, 0.0
                ).astype(jnp.bfloat16)
                picked = jnp.dot(hot, tables[g][...], preferred_element_type=jnp.float32)
                product = picked if product is None else product * picked
            design[pl.ds(at, tile), :] = product.astype(jnp.bfloat16)
            return 0

        lax.fori_loop(0, width // tile, build_tile, 0)

    def transposed_all(left_rows, norm, phase, send, recv, build):
        left_cast = left_rows.astype(jnp.bfloat16)

        def one(step, _):
            q = lax.rem(me + step, n)
            if build:
                build_chunk(q)
            at = pl.multiple_of(q * width, width)
            chunk = lax.dot_general(
                left_cast, design[pl.ds(at, width), :], (((1,), (1,)), ((), ())),
                preferred_element_type=jnp.float32,
            )
            chunk = jnp.where(last, norm, chunk)

            @pl.when(step < n)
            def _():
                send[q] = chunk
                remote(
                    send.at[q], recv.at[me], rs_send.at[phase, q], rs_recv.at[phase, me], {"samples": q}
                ).start()

            @pl.when(step == n)
            def _():
                recv[me] = chunk

            return 0

        lax.fori_loop(1, n + 1, one, 0)

        def arrived(step, _):
            q = lax.rem(me + step, n)
            copy = remote(
                send.at[q], recv.at[q], rs_send.at[phase, q], rs_recv.at[phase, q], {"samples": q}
            )
            copy.wait_recv()
            copy.wait_send()
            return 0

        lax.fori_loop(1, n, arrived, 0)
        return lax.fori_loop(0, n, lambda q, acc: acc + recv[q], jnp.zeros((FIELDS, width), jnp.float32))

    def gather(mine, phase, blocks):
        blocks[me] = mine

        def start(step, _):
            q = lax.rem(me + step, n)
            remote(
                blocks.at[me], blocks.at[me], ag_send.at[phase, q], ag_recv.at[phase, me], {"samples": q}
            ).start()
            return 0

        def finish(step, _):
            q = lax.rem(me + step, n)
            copy = remote(
                blocks.at[me], blocks.at[q], ag_send.at[phase, q], ag_recv.at[phase, q], {"samples": q}
            )
            copy.wait_recv()
            copy.wait_send()
            return 0

        lax.fori_loop(1, n, start, 0)
        lax.fori_loop(1, n, finish, 0)

    def term_norm(phase, blocks):
        half = lax.fori_loop(
            0, n, lambda q, acc: acc + blocks[q][:, width - 1:width], jnp.zeros((FIELDS, 1), jnp.float32)
        )
        norm_out[phase] = jnp.broadcast_to(half, (FIELDS, 128))
        copy = remote(
            norm_out.at[phase], norm_in.at[phase], norm_send.at[phase], norm_recv.at[phase], {"terms": 1 - core}
        )
        copy.start()
        copy.wait()
        return jnp.sqrt(half + norm_in[phase][:, 0:1] + EPS)

    def row_product(phase, blocks, alpha):
        def one(q, acc):
            right = blocks[q] / alpha
            blocks[q] = right
            at = pl.multiple_of(q * width, width)
            return acc + jnp.dot(
                right.astype(jnp.bfloat16), design[pl.ds(at, width), :], preferred_element_type=jnp.float32
            )

        mine = lax.fori_loop(0, n, one, jnp.zeros((FIELDS, rows), jnp.float32))
        cross_out[phase] = mine
        copy = remote(
            cross_out.at[phase], cross_in.at[phase], cross_send.at[phase], cross_recv.at[phase], {"terms": 1 - core}
        )
        copy.start()
        copy.wait()
        return mine + cross_in[phase]

    summed = transposed_all(row_scale * rhs, row_sums(rhs), 0, send1, recv1, True)
    beta = jnp.sqrt(summed[:, width - 1:width] + EPS)
    left = rhs / beta
    raw = jnp.where(last, 0.0, summed) / beta
    gather(jnp.where(last, row_sums(raw), raw), 0, all1)
    alpha = term_norm(0, all1)
    phibar = beta
    rhobar = alpha

    partial = row_scale * row_product(0, all1, alpha) - alpha * left
    summed = transposed_all(row_scale * partial, row_sums(partial), 1, send2, recv2, False)
    beta = jnp.sqrt(summed[:, width - 1:width] + EPS)
    left = partial / beta
    raw = jnp.where(last, 0.0, summed / beta - beta * all1[me])
    gather(jnp.where(last, row_sums(raw), raw), 1, all2)
    alpha = term_norm(1, all2)
    rho = jnp.sqrt(rhobar * rhobar + beta * beta)
    cosine = rhobar / rho
    sine = beta / rho
    theta = sine * alpha
    rhobar = -cosine * alpha
    first = cosine * phibar / rho
    turn = theta / rho
    phibar = sine * phibar

    partial = row_scale * row_product(1, all2, alpha) - alpha * left
    total_in[me] = jnp.broadcast_to(row_sums(partial), (FIELDS, 128))

    def start_total(step, _):
        q = lax.rem(me + step, n)
        remote(total_in.at[me], total_in.at[me], tot_send.at[q], tot_recv.at[me], {"samples": q}).start()
        return 0

    def finish_total(step, _):
        q = lax.rem(me + step, n)
        copy = remote(total_in.at[me], total_in.at[q], tot_send.at[q], tot_recv.at[q], {"samples": q})
        copy.wait_recv()
        copy.wait_send()
        return 0

    lax.fori_loop(1, n, start_total, 0)
    lax.fori_loop(1, n, finish_total, 0)
    square = lax.fori_loop(
        0, n, lambda q, acc: acc + total_in[q][:, 0:1], jnp.zeros((FIELDS, 1), jnp.float32)
    )
    beta = jnp.sqrt(square + EPS)
    left_ref[...] = partial / beta
    rho = jnp.sqrt(rhobar * rhobar + beta * beta)
    second = rhobar / rho * phibar / rho

    def combine(q, _):
        direction = all1[q]
        coeffs_ref[q] = first * direction + second * (all2[q] - turn * direction)
        return 0

    lax.fori_loop(0, n, combine, 0)


def per_device(sample_points, observed, multi_index):
    n = lax.axis_size("samples")
    cores = lax.axis_size("terms")
    rows = sample_points.shape[0]
    inverse_root = 1.0 / math.sqrt(rows * n)
    share = TERMS // cores
    held = -(-share // n)
    width = -(-(held + 1) // 128) * 128
    picks, entries = constants()

    my_terms = lax.dynamic_slice_in_dim(multi_index, lax.axis_index("terms") * share, share, 0)
    powers = np.zeros((INPUTS, 8), np.int32)
    for g, (inputs, _) in enumerate(GROUPS):
        for i, source in enumerate(inputs):
            powers[source, g] = (DEGREE + 1) ** i
    keys = jnp.sum(my_terms[:, :, None] * powers[None], axis=1)
    keys = jnp.pad(keys, ((0, held * n - share), (0, 0)), constant_values=-1)
    keys = jnp.pad(keys.reshape(n, held, 8), ((0, 0), (0, width - held), (0, 0)), constant_values=-1)
    keys = keys.reshape(n * width, 8)
    points = jnp.pad(sample_points.T, ((0, PAD_INPUTS - INPUTS), (0, 0)))

    blocks = (n, FIELDS, width)
    vmem = pl.BlockSpec(memory_space=pltpu.VMEM)
    dma = pltpu.SemaphoreType.DMA
    f32 = jnp.float32
    coeffs, left = pl.pallas_call(
        functools.partial(fit_kernel, n, width, share, inverse_root),
        out_shape=(
            jax.ShapeDtypeStruct(blocks, f32),
            jax.ShapeDtypeStruct((FIELDS, rows), f32),
        ),
        in_specs=[vmem] * 5,
        out_specs=(vmem, vmem),
        scratch_shapes=[
            pltpu.VMEM((n * width, rows), jnp.bfloat16),
            *(pltpu.VMEM((table_width, rows), jnp.bfloat16) for _, table_width in GROUPS),
            *(pltpu.VMEM(blocks, f32) for _ in range(6)),
            pltpu.VMEM((2, FIELDS, rows), f32),
            pltpu.VMEM((2, FIELDS, rows), f32),
            pltpu.VMEM((2, FIELDS, 128), f32),
            pltpu.VMEM((2, FIELDS, 128), f32),
            pltpu.VMEM((n, FIELDS, 128), f32),
            dma((2, n)), dma((2, n)), dma((2, n)), dma((2, n)),
            dma((2,)), dma((2,)), dma((2,)), dma((2,)),
            dma((n,)), dma((n,)),
        ],
        compiler_params=pltpu.CompilerParams(
            collective_id=0, has_side_effects=True, vmem_limit_bytes=48 * 1024 * 1024
        ),
    )(points, observed.T, keys, jnp.asarray(picks, jnp.bfloat16), jnp.asarray(entries))
    coeffs = coeffs.transpose(0, 2, 1)[:, :held, :].reshape(held * n, FIELDS)[:share]
    return coeffs, left.T


def solution(mesh):
    in_specs = (P(("groups", "samples"), None), P(("groups", "samples"), None), P())
    out_specs = (P(("groups", "terms"), None), P(("groups", "samples"), None))
    return jax.shard_map(
        per_device, mesh=mesh, in_specs=in_specs, out_specs=out_specs, check_vma=False
    )
```

time: 341 us -> 106 us (0.31)
  waiting for transfers between devices: 142 us -> 0 us
  Pallas kernels: 0 us -> 98 us
  matrix products: 88.9 us -> 0 us
  blocking collectives: 74.4 us -> 0 us
  between operations: 13.8 us -> 0.73 us
  other arithmetic: 12 us -> 0.87 us
    psum x4 -> x0, waiting for transfers between devices: 142 us -> none  [the longest x2 108 us: term_product(): lax.psum(transposed(design, left_rows.astype(jnp.bfloat16)), 'samples')]
    pallas_call x0 -> x1, Pallas kernels: none -> 98 us  [per_device(): pl.pallas_call(functools.partial(fit_kernel, n, width, share, inverse_roo...]
    dot_general x24 -> x0, matrix products: 88.9 us -> none  [the longest x20 72.4 us: one_block(): jnp.dot(pair_table[:, pair_index, :], selectors[pair_index], precision=la...]
    psum x6 -> x0, blocking collectives: 74.4 us -> none  [the longest x3 66.7 us: row_total(): return lax.psum(column_sums, 'samples')]
    reduce_sum x9 -> x1, other arithmetic: 7.31 us -> 0.87 us  [per_device(): keys = jnp.sum(my_terms[:, :, None] * powers[None], axis=1)]
    while x1 -> x0, local copies, waits for them, and re-layouts: 6.41 us -> none  [build(): lax.map(one_block, points.reshape(row_count // block_rows, block_rows, po...]
    unnamed x4 -> x12, local copies, waits for them, and re-layouts: 0.01 us -> 3.55 us
  transfers between devices with their start and end apart: 4 -> 0, of which waited for: 4 -> 0; matrix products, arithmetic and copies ran while one was open for 0% -> 0% of each run, Pallas kernels for 0% -> 0%
where the time goes in v1:
time: 106 us; the launch traced here: 105 us
  Pallas kernels  98 us (92%)
  local copies, waits for them, and re-layouts  5.75 us (5%)
    pallas_call x1, Pallas kernels, per_device(): pl.pallas_call(functools.partial(fit_kernel, n, width, share, inverse_roo...  98 us
    unnamed x12, local copies, waits for them, and re-layouts  3.55 us

profile of v1, /device:TPU:0, one launch (start us, length us, event | category | flops | bytes accessed | tf_op | source)
XLA Modules:
  0.0 105.4 jit_solution(2042963655315881311)
XLA Ops:
  0.6 0.0 copy-start
  0.6 1.0 copy-done
  1.7 0.1 constant_dynamic-slice_fusion
  1.8 0.9 multiply_reduce_fusion
  2.7 0.1 reshape.14
  2.8 0.6 copy.14
  3.5 0.0 copy-start.4
  3.5 0.0 copy-start.1
  3.5 0.0 copy-start.2
  3.5 0.0 copy-start.3
  3.5 0.1 pad.14.clone
  3.7 0.6 copy-done.4
  4.2 0.7 copy-done.1
  4.9 0.0 copy-done.2
  4.9 0.0 copy-done.3
  4.9 98.0 %shard_map.77 = (f32[8,48,512]{2,1,0:T(8,128)S(1)}, f32[48,512]{1,0:T(8,128)S(1)}) custom-call(f32[16,512]{1,0:T(8,128)S(1)} %pad.12.points_ref, f32[48,512]{1,0:T(8,128)S(1)} %bitcast.14, s32[4096,8]{1,0:T(8,128)S(1)} %bitcast.11, bf16[2048,336]{1,0:T(8,128)(2,1)S(1)} %copy-done.1, s32[8,256]{1,0:T(8,128)S(1)} %copy-done.3), custom_call_target="tpu_custom_call" | custom-call | tf_op jit(solution)/shard_map/pallas_call | solution.py:329
  102.9 0.5 copy.13
  103.4 1.3 %reshape.16 = f32[4008,48]{0,1:T(8,128)} reshape(f32[8,501,48]{1,0,2:T(8,128)S(1)} %copy.13) | data formatting | bytes 1539072 | tf_op jit(solution)/shard_map/reshape | solution.py:354
  104.8 0.6 copy.16
  (2 shorter events, 0.0 us)
Async XLA Ops:
  0.6 1.0 copy-start
  3.5 0.8 copy-start.4
  3.5 1.4 %copy-start.1 = (bf16[2048,336]{1,0:T(8,128)(2,1)S(1)}, bf16[2048,336]{1,0:T(8,128)(2,1)}, u32[]{:S(2)}) copy-start(bf16[2048,336]{1,0:T(8,128)(2,1)} %constant.21.clone.picks_ref) | copy-start | bytes 4128772
  3.5 1.4 %copy-start.2 = (f32[512,48]{0,1:T(8,128)S(1)}, f32[512,48]{0,1:T(8,128)}, u32[]{:S(2)}) copy-start(f32[512,48]{0,1:T(8,128)} %param.7) | copy-start | bytes 294916
  3.5 1.4 %copy-start.3 = (s32[8,256]{1,0:T(8,128)S(1)}, s32[8,256]{1,0:T(8,128)}, u32[]{:S(2)}) copy-start(s32[8,256]{1,0:T(8,128)} %constant.22.clone.entries_ref) | copy-start | bytes 24580

commit v2 on v1

--- a/solution.py
+++ b/solution.py
@@ -58,8 +58,8 @@
     n, width, share, inverse_root,
     points_ref, observed_ref, keys_ref, picks_ref, entries_ref,
     coeffs_ref, left_ref,
-    design, t0, t1, t2, t3, send1, recv1, all1, send2, recv2, all2, cross_out, cross_in, norm_out, norm_in, total_in,
-    rs_send, rs_recv, ag_send, ag_recv, cross_send, cross_recv, norm_send, norm_recv, tot_send, tot_recv,
+    design, t0, t1, t2, t3, send1, met1, recv1, all1, send2, met2, recv2, all2, cross_out, cross_in, norm_out, norm_in, total_in,
+    pair_send, pair_recv, rs_send, rs_recv, ag_send, fw_send, ag_recv, cross_send, cross_recv, norm_send, norm_recv, tot_send, tot_recv,
 ):
     me = lax.axis_index("samples")
     core = lax.axis_index("terms")
@@ -150,11 +150,15 @@
 
         lax.fori_loop(0, width // tile, build_tile, 0)
 
-    def transposed_all(left_rows, norm, phase, send, recv, build):
+    half = n // 2
+    mine_h = me // 2
+    mine_p = lax.rem(me, 2)
+    across = 2 * mine_h + 1 - mine_p
+
+    def transposed_all(left_rows, norm, phase, send, met, recv, build):
         left_cast = left_rows.astype(jnp.bfloat16)
 
-        def one(step, _):
-            q = lax.rem(me + step, n)
+        def partial_chunk(q):
             if build:
                 build_chunk(q)
             at = pl.multiple_of(q * width, width)
@@ -162,68 +166,116 @@
                 left_cast, design[pl.ds(at, width), :], (((1,), (1,)), ((), ())),
                 preferred_element_type=jnp.float32,
             )
-            chunk = jnp.where(last, norm, chunk)
-
-            @pl.when(step < n)
+            return jnp.where(last, norm, chunk)
+
+        def pair_copy(h):
+            return remote(
+                send.at[2 * h + 1 - mine_p], met.at[h],
+                pair_send.at[phase, h], pair_recv.at[phase, h], {"samples": across},
+            )
+
+        def to_pair(step, _):
+            h = lax.rem(mine_h + step, half)
+            send[2 * h + 1 - mine_p] = partial_chunk(2 * h + 1 - mine_p)
+            pair_copy(h).start()
+            return 0
+
+        lax.fori_loop(1, half + 1, to_pair, 0)
+
+        def to_owner(step, _):
+            h = lax.rem(mine_h + step, half)
+            q = 2 * h + mine_p
+            chunk = partial_chunk(q)
+            pair_copy(h).wait_recv()
+            chunk = chunk + met[h]
+
+            @pl.when(step < half)
             def _():
                 send[q] = chunk
                 remote(
-                    send.at[q], recv.at[me], rs_send.at[phase, q], rs_recv.at[phase, me], {"samples": q}
+                    send.at[q], recv.at[mine_h], rs_send.at[phase, h], rs_recv.at[phase, mine_h], {"samples": q}
                 ).start()
 
-            @pl.when(step == n)
+            @pl.when(step == half)
             def _():
-                recv[me] = chunk
-
-            return 0
-
-        lax.fori_loop(1, n + 1, one, 0)
+                recv[mine_h] = chunk
+
+            return 0
+
+        lax.fori_loop(1, half + 1, to_owner, 0)
 
         def arrived(step, _):
-            q = lax.rem(me + step, n)
+            h = lax.rem(mine_h + step, half)
+            q = 2 * h + mine_p
             copy = remote(
-                send.at[q], recv.at[q], rs_send.at[phase, q], rs_recv.at[phase, q], {"samples": q}
+                send.at[q], recv.at[h], rs_send.at[phase, h], rs_recv.at[phase, h], {"samples": q}
             )
             copy.wait_recv()
             copy.wait_send()
             return 0
 
-        lax.fori_loop(1, n, arrived, 0)
-        return lax.fori_loop(0, n, lambda q, acc: acc + recv[q], jnp.zeros((FIELDS, width), jnp.float32))
+        def pair_sent(h, _):
+            pair_copy(h).wait_send()
+            return 0
+
+        lax.fori_loop(1, half, arrived, 0)
+        lax.fori_loop(0, half, pair_sent, 0)
+        return lax.fori_loop(0, half, lambda h, acc: acc + recv[h], jnp.zeros((FIELDS, width), jnp.float32))
 
     def gather(mine, phase, blocks):
         blocks[me] = mine
 
+        def forward(h):
+            q = 2 * h + mine_p
+            return remote(
+                blocks.at[q], blocks.at[q], fw_send.at[phase, h], ag_recv.at[phase, q], {"samples": across}
+            )
+
+        def spread(h, slot):
+            return remote(
+                blocks.at[me], blocks.at[slot], ag_send.at[phase, h], ag_recv.at[phase, slot],
+                {"samples": 2 * h + mine_p},
+            )
+
         def start(step, _):
-            q = lax.rem(me + step, n)
+            spread(lax.rem(mine_h + step, half), me).start()
+            return 0
+
+        def hand_on(step, _):
+            h = lax.rem(mine_h + half - step, half)
+            spread(h, 2 * h + mine_p).wait_recv()
+            forward(h).start()
+            return 0
+
+        def finish(h, _):
+            q = 2 * h + 1 - mine_p
             remote(
-                blocks.at[me], blocks.at[me], ag_send.at[phase, q], ag_recv.at[phase, me], {"samples": q}
-            ).start()
-            return 0
-
-        def finish(step, _):
-            q = lax.rem(me + step, n)
-            copy = remote(
-                blocks.at[me], blocks.at[q], ag_send.at[phase, q], ag_recv.at[phase, q], {"samples": q}
-            )
-            copy.wait_recv()
-            copy.wait_send()
-            return 0
-
-        lax.fori_loop(1, n, start, 0)
-        lax.fori_loop(1, n, finish, 0)
+                blocks.at[q], blocks.at[q], fw_send.at[phase, h], ag_recv.at[phase, q], {"samples": across}
+            ).wait_recv()
+            forward(h).wait_send()
+            return 0
+
+        def sent(step, _):
+            spread(lax.rem(mine_h + step, half), me).wait_send()
+            return 0
+
+        forward(mine_h).start()
+        lax.fori_loop(1, half, start, 0)
+        lax.fori_loop(1, half, hand_on, 0)
+        lax.fori_loop(0, half, finish, 0)
+        lax.fori_loop(1, half, sent, 0)
 
     def term_norm(phase, blocks):
-        half = lax.fori_loop(
+        square = lax.fori_loop(
             0, n, lambda q, acc: acc + blocks[q][:, width - 1:width], jnp.zeros((FIELDS, 1), jnp.float32)
         )
-        norm_out[phase] = jnp.broadcast_to(half, (FIELDS, 128))
+        norm_out[phase] = jnp.broadcast_to(square, (FIELDS, 128))
         copy = remote(
             norm_out.at[phase], norm_in.at[phase], norm_send.at[phase], norm_recv.at[phase], {"terms": 1 - core}
         )
         copy.start()
         copy.wait()
-        return jnp.sqrt(half + norm_in[phase][:, 0:1] + EPS)
+        return jnp.sqrt(square + norm_in[phase][:, 0:1] + EPS)
 
     def row_product(phase, blocks, alpha):
         def one(q, acc):
@@ -243,7 +295,7 @@
         copy.wait()
         return mine + cross_in[phase]
 
-    summed = transposed_all(row_scale * rhs, row_sums(rhs), 0, send1, recv1, True)
+    summed = transposed_all(row_scale * rhs, row_sums(rhs), 0, send1, met1, recv1, True)
     beta = jnp.sqrt(summed[:, width - 1:width] + EPS)
     left = rhs / beta
     raw = jnp.where(last, 0.0, summed) / beta
@@ -253,7 +305,7 @@
     rhobar = alpha
 
     partial = row_scale * row_product(0, all1, alpha) - alpha * left
-    summed = transposed_all(row_scale * partial, row_sums(partial), 1, send2, recv2, False)
+    summed = transposed_all(row_scale * partial, row_sums(partial), 1, send2, met2, recv2, False)
     beta = jnp.sqrt(summed[:, width - 1:width] + EPS)
     left = partial / beta
     raw = jnp.where(last, 0.0, summed / beta - beta * all1[me])
@@ -337,13 +389,13 @@
         scratch_shapes=[
             pltpu.VMEM((n * width, rows), jnp.bfloat16),
             *(pltpu.VMEM((table_width, rows), jnp.bfloat16) for _, table_width in GROUPS),
-            *(pltpu.VMEM(blocks, f32) for _ in range(6)),
+            *(pltpu.VMEM((count, FIELDS, width), f32) for count in (n, n // 2, n // 2, n) * 2),
             pltpu.VMEM((2, FIELDS, rows), f32),
             pltpu.VMEM((2, FIELDS, rows), f32),
             pltpu.VMEM((2, FIELDS, 128), f32),
             pltpu.VMEM((2, FIELDS, 128), f32),
             pltpu.VMEM((n, FIELDS, 128), f32),
-            dma((2, n)), dma((2, n)), dma((2, n)), dma((2, n)),
+            *(dma((2, n // 2)) for _ in range(6)), dma((2, n)),
             dma((2,)), dma((2,)), dma((2,)), dma((2,)),
             dma((n,)), dma((n,)),
         ],

time: 106 us -> 94 us (0.89)
  Pallas kernels: 98 us -> 86.4 us
    pallas_call x1, Pallas kernels: 98 us -> 86.4 us  [per_device(): pl.pallas_call(functools.partial(fit_kernel, n, width, share, inverse_roo...]
where the time goes in v2:
time: 94 us; the launch traced here: 93.7 us
  Pallas kernels  86.4 us (92%)
  local copies, waits for them, and re-layouts  5.75 us (6%)
    pallas_call x1, Pallas kernels, per_device(): pl.pallas_call(functools.partial(fit_kernel, n, width, share, inverse_roo...  86.4 us
    unnamed x12, local copies, waits for them, and re-layouts  3.55 us

profile of v2, /device:TPU:0, one launch (start us, length us, event | category | flops | bytes accessed | tf_op | source)
XLA Modules:
  0.0 93.7 jit_solution(16018440443562176720)
XLA Ops:
  0.6 0.0 copy-start
  0.6 1.0 %copy-done = s32[8008,10]{0,1:T(8,128)S(1)} copy-done((s32[8008,10]{0,1:T(8,128)S(1)}, s32[8008,10]{0,1:T(8,128)}, u32[]{:S(2)}) %copy-start) | copy-done | bytes 320344
  1.7 0.1 constant_dynamic-slice_fusion
  1.8 0.9 multiply_reduce_fusion
  2.7 0.1 reshape.14
  2.8 0.6 copy.14
  3.5 0.0 copy-start.4
  3.5 0.0 copy-start.1
  3.5 0.0 copy-start.2
  3.5 0.0 copy-start.3
  3.5 0.1 pad.14.clone
  3.7 0.6 copy-done.4
  4.2 0.7 copy-done.1
  4.9 0.0 copy-done.2
  4.9 0.0 copy-done.3
  4.9 86.4 %shard_map.77 = (f32[8,48,512]{2,1,0:T(8,128)S(1)}, f32[48,512]{1,0:T(8,128)S(1)}) custom-call(f32[16,512]{1,0:T(8,128)S(1)} %pad.12.points_ref, f32[48,512]{1,0:T(8,128)S(1)} %bitcast.14, s32[4096,8]{1,0:T(8,128)S(1)} %bitcast.11, bf16[2048,336]{1,0:T(8,128)(2,1)S(1)} %copy-done.1, s32[8,256]{1,0:T(8,128)S(1)} %copy-done.3), custom_call_target="tpu_custom_call" | custom-call | tf_op jit(solution)/shard_map/pallas_call | solution.py:381
  91.3 0.5 copy.13
  91.7 1.3 %reshape.16 = f32[4008,48]{0,1:T(8,128)} reshape(f32[8,501,48]{1,0,2:T(8,128)S(1)} %copy.13) | data formatting | bytes 1539072 | tf_op jit(solution)/shard_map/reshape | solution.py:406
  93.1 0.6 copy.16
  (2 shorter events, 0.0 us)
Async XLA Ops:
  0.6 1.0 %copy-start = (s32[8008,10]{0,1:T(8,128)S(1)}, s32[8008,10]{0,1:T(8,128)}, u32[]{:S(2)}) copy-start(s32[8008,10]{0,1:T(8,128)} %param.8) | copy-start | bytes 960964
  3.5 0.8 copy-start.4
  3.5 1.4 %copy-start.1 = (bf16[2048,336]{1,0:T(8,128)(2,1)S(1)}, bf16[2048,336]{1,0:T(8,128)(2,1)}, u32[]{:S(2)}) copy-start(bf16[2048,336]{1,0:T(8,128)(2,1)} %constant.21.clone.picks_ref) | copy-start | bytes 4128772
  3.5 1.4 %copy-start.2 = (f32[512,48]{0,1:T(8,128)S(1)}, f32[512,48]{0,1:T(8,128)}, u32[]{:S(2)}) copy-start(f32[512,48]{0,1:T(8,128)} %param.7) | copy-start | bytes 294916
  3.5 1.4 %copy-start.3 = (s32[8,256]{1,0:T(8,128)S(1)}, s32[8,256]{1,0:T(8,128)}, u32[]{:S(2)}) copy-start(s32[8,256]{1,0:T(8,128)} %constant.22.clone.entries_ref) | copy-start | bytes 24580

commit v3 on v2

--- a/solution.py
+++ b/solution.py
@@ -56,10 +56,12 @@
 
 def fit_kernel(
     n, width, share, inverse_root,
-    points_ref, observed_ref, keys_ref, picks_ref, entries_ref,
+    points_ref, observed_ref, index_ref, picks_ref, entries_ref,
     coeffs_ref, left_ref,
-    design, t0, t1, t2, t3, send1, met1, recv1, all1, send2, met2, recv2, all2, cross_out, cross_in, norm_out, norm_in, total_in,
-    pair_send, pair_recv, rs_send, rs_recv, ag_send, fw_send, ag_recv, cross_send, cross_recv, norm_send, norm_recv, tot_send, tot_recv,
+    design, keys_ref, t0, t1, t2, t3,
+    send1, met1, recv1, all1, right1, send2, met2, recv2, all2, right2,
+    cross_out, cross_in, small,
+    pair_send, pair_recv, rs_send, rs_recv, ag_send, fw_send, ag_recv, cross_send, cross_recv, small_send, small_recv,
 ):
     me = lax.axis_index("samples")
     core = lax.axis_index("terms")
@@ -69,12 +71,29 @@
     barrier = pltpu.get_barrier_semaphore()
 
     def greet(step, _):
-        pl.semaphore_signal(barrier, inc=1, device_id={"samples": lax.rem(me + step, n)}, device_id_type=MESH)
+        pl.semaphore_signal(
+            barrier, inc=1, device_id={"samples": lax.rem(me + step, n), "terms": core}, device_id_type=MESH
+        )
         return 0
 
+    def greet_other(step, _):
+        pl.semaphore_signal(
+            barrier, inc=1, device_id={"samples": lax.rem(me + step, n), "terms": 1 - core}, device_id_type=MESH
+        )
+        return 0
+
     lax.fori_loop(1, n, greet, 0)
-    pl.semaphore_signal(barrier, inc=1, device_id={"terms": 1 - core}, device_id_type=MESH)
-    pl.semaphore_wait(barrier, n)
+    lax.fori_loop(0, n, greet_other, 0)
+
+    key_row = lax.broadcasted_iota(jnp.int32, keys_ref.shape, 0)
+    keys = jnp.zeros(keys_ref.shape, jnp.int32)
+    for g, (inputs, _) in enumerate(GROUPS):
+        key = None
+        for i, source in enumerate(inputs):
+            part = index_ref[source:source + 1, :] * (DEGREE + 1) ** i
+            key = part if key is None else key + part
+        keys = jnp.where(key_row == g, key, keys)
+    keys_ref[...] = keys.astype(jnp.float32)
 
     x = points_ref[...]
     values = [jnp.ones_like(x), x]
@@ -120,9 +139,6 @@
     row_scale = weights * np.float32(inverse_root)
     rhs = weights * observed_ref[...]
 
-    lane = lax.broadcasted_iota(jnp.int32, (FIELDS, width), 1)
-    last = lane == width - 1
-
     def row_sums(value):
         return jnp.sum(value * value, axis=1, keepdims=True)
 
@@ -132,12 +148,58 @@
             device_id=peer, device_id_type=MESH,
         )
 
+    def small_copies(phase, step, terms):
+        q = lax.rem(me + step, n)
+        mine = core * n + me
+        theirs = terms * n + q
+        out = remote(
+            small.at[phase, mine], small.at[phase, mine],
+            small_send.at[phase, theirs], small_recv.at[phase, mine], {"samples": q, "terms": terms},
+        )
+        into = remote(
+            small.at[phase, mine], small.at[phase, theirs],
+            small_send.at[phase, theirs], small_recv.at[phase, theirs], {"samples": q, "terms": terms},
+        )
+        return out, into
+
+    def tell(phase, column, both):
+        small[phase, core * n + me] = jnp.broadcast_to(column, (FIELDS, 128)).T[0:8, :]
+
+        def start(terms):
+            def one(step, _):
+                small_copies(phase, step, terms)[0].start()
+                return 0
+            return one
+
+        lax.fori_loop(1, n, start(core), 0)
+        if both:
+            lax.fori_loop(0, n, start(1 - core), 0)
+
+    def told(phase, both):
+        def finish(terms):
+            def one(step, _):
+                out, into = small_copies(phase, step, terms)
+                into.wait_recv()
+                out.wait_send()
+                return 0
+            return one
+
+        lax.fori_loop(1, n, finish(core), 0)
+        first_slot, count = core * n, n
+        if both:
+            lax.fori_loop(0, n, finish(1 - core), 0)
+            first_slot, count = 0, 2 * n
+        total = lax.fori_loop(
+            0, count, lambda i, acc: acc + small[phase, first_slot + i], jnp.zeros((8, FIELDS), jnp.float32)
+        )
+        return jnp.broadcast_to(total[0:1, :], (128, FIELDS)).T[:, 0:1]
+
     tile = min(width, 256)
 
     def build_chunk(q):
         def build_tile(i, _):
             at = pl.multiple_of(q * width + i * tile, tile)
-            keys = keys_ref[pl.ds(at, tile), :]
+            keys = keys_ref[:, pl.ds(at, tile)].T
             product = None
             for g, (_, table_width) in enumerate(GROUPS):
                 hot = jnp.where(
@@ -155,18 +217,17 @@
     mine_p = lax.rem(me, 2)
     across = 2 * mine_h + 1 - mine_p
 
-    def transposed_all(left_rows, norm, phase, send, met, recv, build):
+    def transposed_all(left_rows, phase, send, met, recv, build):
         left_cast = left_rows.astype(jnp.bfloat16)
 
         def partial_chunk(q):
             if build:
                 build_chunk(q)
             at = pl.multiple_of(q * width, width)
-            chunk = lax.dot_general(
+            return lax.dot_general(
                 left_cast, design[pl.ds(at, width), :], (((1,), (1,)), ((), ())),
                 preferred_element_type=jnp.float32,
             )
-            return jnp.where(last, norm, chunk)
 
         def pair_copy(h):
             return remote(
@@ -222,8 +283,10 @@
         lax.fori_loop(0, half, pair_sent, 0)
         return lax.fori_loop(0, half, lambda h, acc: acc + recv[h], jnp.zeros((FIELDS, width), jnp.float32))
 
-    def gather(mine, phase, blocks):
-        blocks[me] = mine
+    def gather_product(raw, phase, blocks, rights):
+        norm_phase = 2 * phase + 1
+        blocks[me] = raw
+        tell(norm_phase, row_sums(raw), True)
 
         def forward(h):
             q = 2 * h + mine_p
@@ -241,76 +304,68 @@
             spread(lax.rem(mine_h + step, half), me).start()
             return 0
 
-        def hand_on(step, _):
+        forward(mine_h).start()
+        lax.fori_loop(1, half, start, 0)
+        alpha = jnp.sqrt(told(norm_phase, True) + EPS)
+
+        def product(q, acc):
+            right = blocks[q] / alpha
+            rights[q] = right
+            at = pl.multiple_of(q * width, width)
+            return acc + jnp.dot(
+                right.astype(jnp.bfloat16), design[pl.ds(at, width), :], preferred_element_type=jnp.float32
+            )
+
+        def hand_on(step, acc):
             h = lax.rem(mine_h + half - step, half)
             spread(h, 2 * h + mine_p).wait_recv()
             forward(h).start()
-            return 0
-
-        def finish(h, _):
+            return product(2 * h + mine_p, acc)
+
+        def from_pair(step, acc):
+            h = lax.rem(mine_h + half - step, half)
             q = 2 * h + 1 - mine_p
             remote(
                 blocks.at[q], blocks.at[q], fw_send.at[phase, h], ag_recv.at[phase, q], {"samples": across}
             ).wait_recv()
-            forward(h).wait_send()
-            return 0
+            return product(q, acc)
 
         def sent(step, _):
             spread(lax.rem(mine_h + step, half), me).wait_send()
             return 0
 
-        forward(mine_h).start()
-        lax.fori_loop(1, half, start, 0)
-        lax.fori_loop(1, half, hand_on, 0)
-        lax.fori_loop(0, half, finish, 0)
-        lax.fori_loop(1, half, sent, 0)
-
-    def term_norm(phase, blocks):
-        square = lax.fori_loop(
-            0, n, lambda q, acc: acc + blocks[q][:, width - 1:width], jnp.zeros((FIELDS, 1), jnp.float32)
-        )
-        norm_out[phase] = jnp.broadcast_to(square, (FIELDS, 128))
-        copy = remote(
-            norm_out.at[phase], norm_in.at[phase], norm_send.at[phase], norm_recv.at[phase], {"terms": 1 - core}
-        )
-        copy.start()
-        copy.wait()
-        return jnp.sqrt(square + norm_in[phase][:, 0:1] + EPS)
-
-    def row_product(phase, blocks, alpha):
-        def one(q, acc):
-            right = blocks[q] / alpha
-            blocks[q] = right
-            at = pl.multiple_of(q * width, width)
-            return acc + jnp.dot(
-                right.astype(jnp.bfloat16), design[pl.ds(at, width), :], preferred_element_type=jnp.float32
-            )
-
-        mine = lax.fori_loop(0, n, one, jnp.zeros((FIELDS, rows), jnp.float32))
-        cross_out[phase] = mine
+        def forwarded(h, _):
+            forward(h).wait_send()
+            return 0
+
+        acc = product(me, jnp.zeros((FIELDS, rows), jnp.float32))
+        acc = lax.fori_loop(1, half, hand_on, acc)
+        acc = lax.fori_loop(0, half, from_pair, acc)
+        cross_out[phase] = acc
         copy = remote(
             cross_out.at[phase], cross_in.at[phase], cross_send.at[phase], cross_recv.at[phase], {"terms": 1 - core}
         )
         copy.start()
+        lax.fori_loop(1, half, sent, 0)
+        lax.fori_loop(0, half, forwarded, 0)
         copy.wait()
-        return mine + cross_in[phase]
-
-    summed = transposed_all(row_scale * rhs, row_sums(rhs), 0, send1, met1, recv1, True)
-    beta = jnp.sqrt(summed[:, width - 1:width] + EPS)
+        return alpha, acc + cross_in[phase]
+
+    pl.semaphore_wait(barrier, 2 * n - 1)
+    tell(0, row_sums(rhs), False)
+    summed = transposed_all(row_scale * rhs, 0, send1, met1, recv1, True)
+    beta = jnp.sqrt(told(0, False) + EPS)
     left = rhs / beta
-    raw = jnp.where(last, 0.0, summed) / beta
-    gather(jnp.where(last, row_sums(raw), raw), 0, all1)
-    alpha = term_norm(0, all1)
+    alpha, image = gather_product(summed / beta, 0, all1, right1)
     phibar = beta
     rhobar = alpha
 
-    partial = row_scale * row_product(0, all1, alpha) - alpha * left
-    summed = transposed_all(row_scale * partial, row_sums(partial), 1, send2, met2, recv2, False)
-    beta = jnp.sqrt(summed[:, width - 1:width] + EPS)
+    partial = row_scale * image - alpha * left
+    tell(2, row_sums(partial), False)
+    summed = transposed_all(row_scale * partial, 1, send2, met2, recv2, False)
+    beta = jnp.sqrt(told(2, False) + EPS)
     left = partial / beta
-    raw = jnp.where(last, 0.0, summed / beta - beta * all1[me])
-    gather(jnp.where(last, row_sums(raw), raw), 1, all2)
-    alpha = term_norm(1, all2)
+    alpha, image = gather_product(summed / beta - beta * right1[me], 1, all2, right2)
     rho = jnp.sqrt(rhobar * rhobar + beta * beta)
     cosine = rhobar / rho
     sine = beta / rho
@@ -320,37 +375,17 @@
     turn = theta / rho
     phibar = sine * phibar
 
-    partial = row_scale * row_product(1, all2, alpha) - alpha * left
-    total_in[me] = jnp.broadcast_to(row_sums(partial), (FIELDS, 128))
-
-    def start_total(step, _):
-        q = lax.rem(me + step, n)
-        remote(total_in.at[me], total_in.at[me], tot_send.at[q], tot_recv.at[me], {"samples": q}).start()
-        return 0
-
-    def finish_total(step, _):
-        q = lax.rem(me + step, n)
-        copy = remote(total_in.at[me], total_in.at[q], tot_send.at[q], tot_recv.at[q], {"samples": q})
-        copy.wait_recv()
-        copy.wait_send()
-        return 0
-
-    lax.fori_loop(1, n, start_total, 0)
-    lax.fori_loop(1, n, finish_total, 0)
-    square = lax.fori_loop(
-        0, n, lambda q, acc: acc + total_in[q][:, 0:1], jnp.zeros((FIELDS, 1), jnp.float32)
-    )
-    beta = jnp.sqrt(square + EPS)
+    partial = row_scale * image - alpha * left
+    tell(4, row_sums(partial), False)
+    beta = jnp.sqrt(told(4, False) + EPS)
     left_ref[...] = partial / beta
     rho = jnp.sqrt(rhobar * rhobar + beta * beta)
     second = rhobar / rho * phibar / rho
-
-    def combine(q, _):
-        direction = all1[q]
-        coeffs_ref[q] = first * direction + second * (all2[q] - turn * direction)
-        return 0
-
-    lax.fori_loop(0, n, combine, 0)
+    for q in range(-(-share // width)):
+        at = q * width
+        held = min(width, share - at)
+        direction = right1[q][:, 0:held]
+        coeffs_ref[:, at:at + held] = first * direction + second * (right2[q][:, 0:held] - turn * direction)
 
 
 def per_device(sample_points, observed, multi_index):
@@ -359,52 +394,42 @@
     rows = sample_points.shape[0]
     inverse_root = 1.0 / math.sqrt(rows * n)
     share = TERMS // cores
-    held = -(-share // n)
-    width = -(-(held + 1) // 128) * 128
+    width = -(-share // (n * 128)) * 128
     picks, entries = constants()
 
-    my_terms = lax.dynamic_slice_in_dim(multi_index, lax.axis_index("terms") * share, share, 0)
-    powers = np.zeros((INPUTS, 8), np.int32)
-    for g, (inputs, _) in enumerate(GROUPS):
-        for i, source in enumerate(inputs):
-            powers[source, g] = (DEGREE + 1) ** i
-    keys = jnp.sum(my_terms[:, :, None] * powers[None], axis=1)
-    keys = jnp.pad(keys, ((0, held * n - share), (0, 0)), constant_values=-1)
-    keys = jnp.pad(keys.reshape(n, held, 8), ((0, 0), (0, width - held), (0, 0)), constant_values=-1)
-    keys = keys.reshape(n * width, 8)
+    my_terms = lax.dynamic_slice_in_dim(multi_index.T, lax.axis_index("terms") * share, share, 1)
+    my_terms = jnp.pad(
+        my_terms, ((0, PAD_INPUTS - INPUTS), (0, n * width - share)), constant_values=-1
+    )
     points = jnp.pad(sample_points.T, ((0, PAD_INPUTS - INPUTS), (0, 0)))
 
-    blocks = (n, FIELDS, width)
     vmem = pl.BlockSpec(memory_space=pltpu.VMEM)
     dma = pltpu.SemaphoreType.DMA
     f32 = jnp.float32
     coeffs, left = pl.pallas_call(
         functools.partial(fit_kernel, n, width, share, inverse_root),
         out_shape=(
-            jax.ShapeDtypeStruct(blocks, f32),
+            jax.ShapeDtypeStruct((FIELDS, share), f32),
             jax.ShapeDtypeStruct((FIELDS, rows), f32),
         ),
         in_specs=[vmem] * 5,
         out_specs=(vmem, vmem),
         scratch_shapes=[
             pltpu.VMEM((n * width, rows), jnp.bfloat16),
+            pltpu.VMEM((8, n * width), f32),
             *(pltpu.VMEM((table_width, rows), jnp.bfloat16) for _, table_width in GROUPS),
-            *(pltpu.VMEM((count, FIELDS, width), f32) for count in (n, n // 2, n // 2, n) * 2),
+            *(pltpu.VMEM((count, FIELDS, width), f32) for count in (n, n // 2, n // 2, n, n) * 2),
             pltpu.VMEM((2, FIELDS, rows), f32),
             pltpu.VMEM((2, FIELDS, rows), f32),
-            pltpu.VMEM((2, FIELDS, 128), f32),
-            pltpu.VMEM((2, FIELDS, 128), f32),
-            pltpu.VMEM((n, FIELDS, 128), f32),
-            *(dma((2, n // 2)) for _ in range(6)), dma((2, n)),
-            dma((2,)), dma((2,)), dma((2,)), dma((2,)),
-            dma((n,)), dma((n,)),
+            pltpu.VMEM((5, 2 * n, 8, FIELDS), f32),
+            *(dma((2, n // 2)) for _ in range(6)), dma((2, n)), dma((2,)), dma((2,)),
+            dma((5, 2 * n)), dma((5, 2 * n)),
         ],
         compiler_params=pltpu.CompilerParams(
             collective_id=0, has_side_effects=True, vmem_limit_bytes=48 * 1024 * 1024
         ),
-    )(points, observed.T, keys, jnp.asarray(picks, jnp.bfloat16), jnp.asarray(entries))
-    coeffs = coeffs.transpose(0, 2, 1)[:, :held, :].reshape(held * n, FIELDS)[:share]
-    return coeffs, left.T
+    )(points, observed.T, my_terms, jnp.asarray(picks, jnp.bfloat16), jnp.asarray(entries, f32))
+    return coeffs.T, left.T
 
 
 def solution(mesh):

time: 94 us -> 92.7 us (0.986)
    reshape x2 -> x0, local copies, waits for them, and re-layouts: 1.47 us -> none  [the longest x1 1.34 us: per_device(): coeffs.transpose(0, 2, 1)[:, :held, :].reshape(held * n, FIELDS)[:share]]
    unnamed x12 -> x10, local copies, waits for them, and re-layouts: 3.55 us -> 4.74 us
where the time goes in v3:
time: 92.7 us; the launch traced here: 92.4 us
  Pallas kernels  86.1 us (93%)
  local copies, waits for them, and re-layouts  5.71 us (6%)
    pallas_call x1, Pallas kernels, per_device(): pl.pallas_call(functools.partial(fit_kernel, n, width, share, inverse_roo...  86.1 us
    unnamed x10, local copies, waits for them, and re-layouts  4.74 us

profile of v3, /device:TPU:0, one launch (start us, length us, event | category | flops | bytes accessed | tf_op | source)
XLA Modules:
  0.0 92.4 jit_solution(4119738854972183090)
XLA Ops:
  0.6 0.0 copy-start
  0.6 0.8 pad.8.points_ref
  1.5 0.2 copy-done
  1.7 0.1 dynamic-slice_bitcast_fusion
  1.9 0.0 copy-start.1
  1.9 1.4 %copy-done.1 = bf16[2048,336]{1,0:T(8,128)(2,1)S(1)} copy-done((bf16[2048,336]{1,0:T(8,128)(2,1)S(1)}, bf16[2048,336]{1,0:T(8,128)(2,1)}, u32[]{:S(2)}) %copy-start.1) | copy-done | bytes 1376280
  3.3 0.0 copy-start.2
  3.3 0.9 copy-done.2
  4.2 0.0 copy-start.3
  4.2 0.7 copy-done.3
  4.9 86.1 %shard_map.68 = (f32[48,4004]{1,0:T(8,128)S(1)}, f32[48,512]{1,0:T(8,128)S(1)}) custom-call(f32[16,512]{1,0:T(8,128)S(1)} %pad.8.points_ref, f32[48,512]{1,0:T(8,128)S(1)} %bitcast.8, s32[16,4096]{1,0:T(8,128)S(1)} %pad.9.index_ref, bf16[2048,336]{1,0:T(8,128)(2,1)S(1)} %copy-done.1, f32[8,256]{1,0:T(8,128)S(1)} %copy-done.3), custom_call_target="tpu_custom_call" | custom-call | tf_op jit(solution)/shard_map/pallas_call | solution.py:409
  90.9 0.9 copy.9
  91.8 0.6 copy.10
  (1 shorter events, 0.0 us)
Async XLA Ops:
  0.6 1.1 %copy-start = (s32[8008,10]{0,1:T(8,128)S(1)}, s32[8008,10]{0,1:T(8,128)}, u32[]{:S(2)}) copy-start(s32[8008,10]{0,1:T(8,128)} %param.7) | copy-start | bytes 960964
  1.9 1.4 %copy-start.1 = (bf16[2048,336]{1,0:T(8,128)(2,1)S(1)}, bf16[2048,336]{1,0:T(8,128)(2,1)}, u32[]{:S(2)}) copy-start(bf16[2048,336]{1,0:T(8,128)(2,1)} %constant.18.clone.picks_ref) | copy-start | bytes 4128772
  3.3 0.9 copy-start.2
  4.2 0.7 copy-start.3

commit v4 on v3

--- a/solution.py
+++ b/solution.py
@@ -54,36 +54,44 @@
     return high, middle, rest - middle
 
 
+def wrap(value, count):
+    return jnp.where(value >= count, value - count, value)
+
+
 def fit_kernel(
     n, width, share, inverse_root,
-    points_ref, observed_ref, index_ref, picks_ref, entries_ref,
+    points_ref, observed_hbm, index_ref, picks_hbm, entries_ref,
     coeffs_ref, left_ref,
     design, keys_ref, t0, t1, t2, t3,
     send1, met1, recv1, all1, right1, send2, met2, recv2, all2, right2,
     cross_out, cross_in, small,
-    pair_send, pair_recv, rs_send, rs_recv, ag_send, fw_send, ag_recv, cross_send, cross_recv, small_send, small_recv,
+    pair_send, pair_recv, rs_send, rs_recv, ag_send, fw_send, ag_recv, cross_send, cross_recv, small_send, small_recv, load_sem,
+    observed_ref, picks_ref,
 ):
     me = lax.axis_index("samples")
     core = lax.axis_index("terms")
     rows = points_ref.shape[1]
+
+    def each(first_step, stop, body, carry=0):
+        return lax.fori_loop(first_step, stop, body, carry, unroll=n <= 8)
+
     tables = (t0, t1, t2, t3)
+
+    load_picks = pltpu.make_async_copy(picks_hbm, picks_ref, load_sem.at[0])
+    load_observed = pltpu.make_async_copy(observed_hbm, observed_ref, load_sem.at[1])
+    load_picks.start()
+    load_observed.start()
 
     barrier = pltpu.get_barrier_semaphore()
 
     def greet(step, _):
         pl.semaphore_signal(
-            barrier, inc=1, device_id={"samples": lax.rem(me + step, n), "terms": core}, device_id_type=MESH
+            barrier, inc=1, device_id={"samples": wrap(me + step, n), "terms": core}, device_id_type=MESH
         )
         return 0
 
-    def greet_other(step, _):
-        pl.semaphore_signal(
-            barrier, inc=1, device_id={"samples": lax.rem(me + step, n), "terms": 1 - core}, device_id_type=MESH
-        )
-        return 0
-
-    lax.fori_loop(1, n, greet, 0)
-    lax.fori_loop(0, n, greet_other, 0)
+    each(1, n, greet, 0)
+    pl.semaphore_signal(barrier, inc=1, device_id={"terms": 1 - core}, device_id_type=MESH)
 
     key_row = lax.broadcasted_iota(jnp.int32, keys_ref.shape, 0)
     keys = jnp.zeros(keys_ref.shape, jnp.int32)
@@ -107,6 +115,7 @@
         parts.extend(p.astype(jnp.bfloat16) for p in pieces_of(v))
     flat = jnp.concatenate(parts, axis=0)
 
+    load_picks.wait()
     offset = 0
     for g, (inputs, table_width) in enumerate(GROUPS):
         table = None
@@ -137,6 +146,7 @@
     squares = functools.reduce(lambda a, b: a + b, poly)
     weights = jnp.sqrt(TERMS / squares)
     row_scale = weights * np.float32(inverse_root)
+    load_observed.wait()
     rhs = weights * observed_ref[...]
 
     def row_sums(value):
@@ -148,53 +158,54 @@
             device_id=peer, device_id_type=MESH,
         )
 
-    def small_copies(phase, step, terms):
-        q = lax.rem(me + step, n)
-        mine = core * n + me
-        theirs = terms * n + q
-        out = remote(
-            small.at[phase, mine], small.at[phase, mine],
-            small_send.at[phase, theirs], small_recv.at[phase, mine], {"samples": q, "terms": terms},
+    def small_copy(phase, step, slot):
+        q = wrap(me + step, n)
+        return remote(
+            small.at[phase, me], small.at[phase, q if slot is None else slot],
+            small_send.at[phase, q], small_recv.at[phase, q if slot is None else slot], {"samples": q},
         )
-        into = remote(
-            small.at[phase, mine], small.at[phase, theirs],
-            small_send.at[phase, theirs], small_recv.at[phase, theirs], {"samples": q, "terms": terms},
-        )
-        return out, into
-
-    def tell(phase, column, both):
-        small[phase, core * n + me] = jnp.broadcast_to(column, (FIELDS, 128)).T[0:8, :]
-
-        def start(terms):
-            def one(step, _):
-                small_copies(phase, step, terms)[0].start()
-                return 0
-            return one
-
-        lax.fori_loop(1, n, start(core), 0)
+
+    def as_row(column):
+        return jnp.broadcast_to(column, (FIELDS, 128)).T[0:8, :]
+
+    def as_column(row):
+        return jnp.broadcast_to(row[0:1, :], (128, FIELDS)).T[:, 0:1]
+
+    def tell(phase, column):
+        small[phase, me] = as_row(column)
+
+        def start(step, _):
+            small_copy(phase, step, me).start()
+            return 0
+
+        each(1, n, start)
+
+    def told(phase, both):
+        def arrive(step, _):
+            small_copy(phase, step, None).wait_recv()
+            return 0
+
+        def leave(step, _):
+            small_copy(phase, step, None).wait_send()
+            return 0
+
+        each(1, n, arrive)
+        total = each(0, n, lambda i, acc: acc + small[phase, i], jnp.zeros((8, FIELDS), jnp.float32))
         if both:
-            lax.fori_loop(0, n, start(1 - core), 0)
-
-    def told(phase, both):
-        def finish(terms):
-            def one(step, _):
-                out, into = small_copies(phase, step, terms)
-                into.wait_recv()
-                out.wait_send()
-                return 0
-            return one
-
-        lax.fori_loop(1, n, finish(core), 0)
-        first_slot, count = core * n, n
-        if both:
-            lax.fori_loop(0, n, finish(1 - core), 0)
-            first_slot, count = 0, 2 * n
-        total = lax.fori_loop(
-            0, count, lambda i, acc: acc + small[phase, first_slot + i], jnp.zeros((8, FIELDS), jnp.float32)
-        )
-        return jnp.broadcast_to(total[0:1, :], (128, FIELDS)).T[:, 0:1]
-
-    tile = min(width, 256)
+            small[phase, n] = total
+            copy = remote(
+                small.at[phase, n], small.at[phase, n + 1],
+                small_send.at[phase, n], small_recv.at[phase, n], {"terms": 1 - core},
+            )
+            copy.start()
+            each(1, n, leave)
+            copy.wait()
+            total = total + small[phase, n + 1]
+        else:
+            each(1, n, leave)
+        return as_column(total)
+
+    tile = min(width, 512)
 
     def build_chunk(q):
         def build_tile(i, _):
@@ -236,7 +247,7 @@
             )
 
         def to_pair(step, _):
-            h = lax.rem(mine_h + step, half)
+            h = wrap(mine_h + step, half)
             send[2 * h + 1 - mine_p] = partial_chunk(2 * h + 1 - mine_p)
             pair_copy(h).start()
             return 0
@@ -244,7 +255,7 @@
         lax.fori_loop(1, half + 1, to_pair, 0)
 
         def to_owner(step, _):
-            h = lax.rem(mine_h + step, half)
+            h = wrap(mine_h + step, half)
             q = 2 * h + mine_p
             chunk = partial_chunk(q)
             pair_copy(h).wait_recv()
@@ -266,7 +277,7 @@
         lax.fori_loop(1, half + 1, to_owner, 0)
 
         def arrived(step, _):
-            h = lax.rem(mine_h + step, half)
+            h = wrap(mine_h + step, half)
             q = 2 * h + mine_p
             copy = remote(
                 send.at[q], recv.at[h], rs_send.at[phase, h], rs_recv.at[phase, h], {"samples": q}
@@ -279,14 +290,14 @@
             pair_copy(h).wait_send()
             return 0
 
-        lax.fori_loop(1, half, arrived, 0)
-        lax.fori_loop(0, half, pair_sent, 0)
-        return lax.fori_loop(0, half, lambda h, acc: acc + recv[h], jnp.zeros((FIELDS, width), jnp.float32))
+        each(1, half, arrived, 0)
+        each(0, half, pair_sent, 0)
+        return each(0, half, lambda h, acc: acc + recv[h], jnp.zeros((FIELDS, width), jnp.float32))
 
     def gather_product(raw, phase, blocks, rights):
         norm_phase = 2 * phase + 1
         blocks[me] = raw
-        tell(norm_phase, row_sums(raw), True)
+        tell(norm_phase, row_sums(raw))
 
         def forward(h):
             q = 2 * h + mine_p
@@ -301,11 +312,11 @@
             )
 
         def start(step, _):
-            spread(lax.rem(mine_h + step, half), me).start()
+            spread(wrap(mine_h + step, half), me).start()
             return 0
 
         forward(mine_h).start()
-        lax.fori_loop(1, half, start, 0)
+        each(1, half, start, 0)
         alpha = jnp.sqrt(told(norm_phase, True) + EPS)
 
         def product(q, acc):
@@ -317,13 +328,13 @@
             )
 
         def hand_on(step, acc):
-            h = lax.rem(mine_h + half - step, half)
+            h = wrap(mine_h + half - step, half)
             spread(h, 2 * h + mine_p).wait_recv()
             forward(h).start()
             return product(2 * h + mine_p, acc)
 
         def from_pair(step, acc):
-            h = lax.rem(mine_h + half - step, half)
+            h = wrap(mine_h + half - step, half)
             q = 2 * h + 1 - mine_p
             remote(
                 blocks.at[q], blocks.at[q], fw_send.at[phase, h], ag_recv.at[phase, q], {"samples": across}
@@ -331,7 +342,7 @@
             return product(q, acc)
 
         def sent(step, _):
-            spread(lax.rem(mine_h + step, half), me).wait_send()
+            spread(wrap(mine_h + step, half), me).wait_send()
             return 0
 
         def forwarded(h, _):
@@ -346,13 +357,13 @@
             cross_out.at[phase], cross_in.at[phase], cross_send.at[phase], cross_recv.at[phase], {"terms": 1 - core}
         )
         copy.start()
-        lax.fori_loop(1, half, sent, 0)
-        lax.fori_loop(0, half, forwarded, 0)
+        each(1, half, sent, 0)
+        each(0, half, forwarded, 0)
         copy.wait()
         return alpha, acc + cross_in[phase]
 
-    pl.semaphore_wait(barrier, 2 * n - 1)
-    tell(0, row_sums(rhs), False)
+    pl.semaphore_wait(barrier, n)
+    tell(0, row_sums(rhs))
     summed = transposed_all(row_scale * rhs, 0, send1, met1, recv1, True)
     beta = jnp.sqrt(told(0, False) + EPS)
     left = rhs / beta
@@ -361,7 +372,7 @@
     rhobar = alpha
 
     partial = row_scale * image - alpha * left
-    tell(2, row_sums(partial), False)
+    tell(2, row_sums(partial))
     summed = transposed_all(row_scale * partial, 1, send2, met2, recv2, False)
     beta = jnp.sqrt(told(2, False) + EPS)
     left = partial / beta
@@ -376,7 +387,7 @@
     phibar = sine * phibar
 
     partial = row_scale * image - alpha * left
-    tell(4, row_sums(partial), False)
+    tell(4, row_sums(partial))
     beta = jnp.sqrt(told(4, False) + EPS)
     left_ref[...] = partial / beta
     rho = jnp.sqrt(rhobar * rhobar + beta * beta)
@@ -412,7 +423,7 @@
             jax.ShapeDtypeStruct((FIELDS, share), f32),
             jax.ShapeDtypeStruct((FIELDS, rows), f32),
         ),
-        in_specs=[vmem] * 5,
+        in_specs=[vmem, pl.BlockSpec(memory_space=pl.ANY), vmem, pl.BlockSpec(memory_space=pl.ANY), vmem],
         out_specs=(vmem, vmem),
         scratch_shapes=[
             pltpu.VMEM((n * width, rows), jnp.bfloat16),
@@ -421,12 +432,14 @@
             *(pltpu.VMEM((count, FIELDS, width), f32) for count in (n, n // 2, n // 2, n, n) * 2),
             pltpu.VMEM((2, FIELDS, rows), f32),
             pltpu.VMEM((2, FIELDS, rows), f32),
-            pltpu.VMEM((5, 2 * n, 8, FIELDS), f32),
+            pltpu.VMEM((5, n + 2, 8, FIELDS), f32),
             *(dma((2, n // 2)) for _ in range(6)), dma((2, n)), dma((2,)), dma((2,)),
-            dma((5, 2 * n)), dma((5, 2 * n)),
+            dma((5, n + 1)), dma((5, n + 1)), dma((2,)),
+            pltpu.VMEM((FIELDS, rows), f32),
+            pltpu.VMEM(picks.shape, jnp.bfloat16),
         ],
         compiler_params=pltpu.CompilerParams(
-            collective_id=0, has_side_effects=True, vmem_limit_bytes=48 * 1024 * 1024
+            collective_id=0, has_side_effects=True, vmem_limit_bytes=56 * 1024 * 1024
         ),
     )(points, observed.T, my_terms, jnp.asarray(picks, jnp.bfloat16), jnp.asarray(entries, f32))
     return coeffs.T, left.T

time: 92.7 us -> 90.9 us (0.981)
  Pallas kernels: 86.1 us -> 85 us
    unnamed x10 -> x6, local copies, waits for them, and re-layouts: 4.74 us -> 2.75 us
    pallas_call x1, Pallas kernels: 86.1 us -> 85 us  [per_device(): pl.pallas_call(functools.partial(fit_kernel, n, width, share, inverse_roo...]
where the time goes in v4:
time: 90.9 us; the launch traced here: 90.7 us
  Pallas kernels  85 us (94%)
  local copies, waits for them, and re-layouts  5.04 us (6%)
    pallas_call x1, Pallas kernels, per_device(): pl.pallas_call(functools.partial(fit_kernel, n, width, share, inverse_roo...  85 us
    unnamed x6, local copies, waits for them, and re-layouts  2.75 us

profile of v4, /device:TPU:0, one launch (start us, length us, event | category | flops | bytes accessed | tf_op | source)
XLA Modules:
  0.0 90.7 jit_solution(7491348243755851346)
XLA Ops:
  0.6 0.0 copy-start
  0.6 1.4 %pad.8.points_ref = f32[16,512]{1,0:T(8,128)} pad(f32[10,512]{1,0:T(8,128)} %bitcast.9, f32[]{:T(128)} %constant.4.clone.1), padding=0_6x0_0 | pad | bytes 53252 | tf_op jit(solution)/shard_map/jit(_pad)/pad | solution.py:415
  2.1 0.0 copy-done
  2.1 0.1 dynamic-slice_bitcast_fusion
  2.2 0.7 pad.9.index_ref
  2.9 85.0 %shard_map.68 = (f32[48,4004]{1,0:T(8,128)}, f32[48,512]{1,0:T(8,128)}) custom-call(f32[16,512]{1,0:T(8,128)} %pad.8.points_ref, f32[48,512]{1,0:T(8,128)} %bitcast.8, s32[16,4096]{1,0:T(8,128)} %pad.9.index_ref, bf16[2048,336]{1,0:T(8,128)(2,1)} %constant.18.clone.picks_hbm, f32[8,256]{1,0:T(8,128)} %constant.19.clone.entries_ref), custom_call_target="tpu_custom_call" | custom-call | tf_op jit(solution)/shard_map/pallas_call | solution.py:420
  87.9 0.0 copy-start.1
  87.9 2.1 %copy.9 = f32[4004,48]{0,1:T(8,128)} copy(f32[4004,48]{0,1:T(8,128)} %bitcast.6) | data formatting | bytes 1537536
  90.0 0.0 copy-done.1
  90.0 0.6 copy.10
Async XLA Ops:
  0.6 1.5 %copy-start = (s32[8008,10]{0,1:T(8,128)S(1)}, s32[8008,10]{0,1:T(8,128)}, u32[]{:S(2)}) copy-start(s32[8008,10]{0,1:T(8,128)} %param.7) | copy-start | bytes 960964
  87.9 2.1 %copy-start.1 = (f32[48,512]{1,0:T(8,128)S(1)}, f32[48,512]{1,0:T(8,128)}, u32[]{:S(2)}) copy-start(f32[48,512]{1,0:T(8,128)} %get-tuple-element.5) | copy-start | bytes 294916

commit v5 on v4

--- a/solution.py
+++ b/solution.py
@@ -229,16 +229,15 @@
     across = 2 * mine_h + 1 - mine_p
 
     def transposed_all(left_rows, phase, send, met, recv, build):
-        left_cast = left_rows.astype(jnp.bfloat16)
+        left_cast = left_rows.T.astype(jnp.bfloat16)
 
         def partial_chunk(q):
             if build:
                 build_chunk(q)
             at = pl.multiple_of(q * width, width)
-            return lax.dot_general(
-                left_cast, design[pl.ds(at, width), :], (((1,), (1,)), ((), ())),
-                preferred_element_type=jnp.float32,
-            )
+            return jnp.dot(
+                design[pl.ds(at, width), :], left_cast, preferred_element_type=jnp.float32
+            ).T
 
         def pair_copy(h):
             return remote(
@@ -439,7 +438,7 @@
             pltpu.VMEM(picks.shape, jnp.bfloat16),
         ],
         compiler_params=pltpu.CompilerParams(
-            collective_id=0, has_side_effects=True, vmem_limit_bytes=56 * 1024 * 1024
+            collective_id=0, has_side_effects=True, vmem_limit_bytes=44 * 1024 * 1024
         ),
     )(points, observed.T, my_terms, jnp.asarray(picks, jnp.bfloat16), jnp.asarray(entries, f32))
     return coeffs.T, left.T

time: 90.9 us -> 89.3 us (0.982)
  Pallas kernels: 85 us -> 82.7 us
    pallas_call x1, Pallas kernels: 85 us -> 82.7 us  [per_device(): pl.pallas_call(functools.partial(fit_kernel, n, width, share, inverse_roo...]
    unnamed x6 -> x10, local copies, waits for them, and re-layouts: 2.75 us -> 4.74 us
where the time goes in v5:
time: 89.3 us; the launch traced here: 89 us
  Pallas kernels  82.7 us (93%)
  local copies, waits for them, and re-layouts  5.71 us (6%)
    pallas_call x1, Pallas kernels, per_device(): pl.pallas_call(functools.partial(fit_kernel, n, width, share, inverse_roo...  82.7 us
    unnamed x10, local copies, waits for them, and re-layouts  4.74 us

profile of v5, /device:TPU:0, one launch (start us, length us, event | category | flops | bytes accessed | tf_op | source)
XLA Modules:
  0.0 89.0 jit_solution(13625102387000239778)
XLA Ops:
  0.6 0.0 copy-start
  0.6 0.8 pad.8.points_ref
  1.5 0.2 copy-done
  1.7 0.1 dynamic-slice_bitcast_fusion
  1.9 0.0 copy-start.1
  1.9 1.4 %copy-done.1 = bf16[2048,336]{1,0:T(8,128)(2,1)S(1)} copy-done((bf16[2048,336]{1,0:T(8,128)(2,1)S(1)}, bf16[2048,336]{1,0:T(8,128)(2,1)}, u32[]{:S(2)}) %copy-start.1) | copy-done | bytes 1376280
  3.3 0.0 copy-start.2
  3.3 0.9 %copy-done.2 = f32[512,48]{0,1:T(8,128)S(1)} copy-done((f32[512,48]{0,1:T(8,128)S(1)}, f32[512,48]{0,1:T(8,128)}, u32[]{:S(2)}) %copy-start.2) | copy-done | bytes 98328
  4.2 0.0 copy-start.3
  4.2 0.7 copy-done.3
  4.9 82.7 %shard_map.68 = (f32[48,4004]{1,0:T(8,128)S(1)}, f32[48,512]{1,0:T(8,128)S(1)}) custom-call(f32[16,512]{1,0:T(8,128)S(1)} %pad.8.points_ref, f32[48,512]{1,0:T(8,128)S(1)} %bitcast.8, s32[16,4096]{1,0:T(8,128)S(1)} %pad.9.index_ref, bf16[2048,336]{1,0:T(8,128)(2,1)S(1)} %copy-done.1, f32[8,256]{1,0:T(8,128)S(1)} %copy-done.3), custom_call_target="tpu_custom_call" | custom-call | tf_op jit(solution)/shard_map/pallas_call | solution.py:419
  87.5 0.9 copy.9
  88.4 0.6 copy.10
  (1 shorter events, 0.0 us)
Async XLA Ops:
  0.6 1.1 %copy-start = (s32[8008,10]{0,1:T(8,128)S(1)}, s32[8008,10]{0,1:T(8,128)}, u32[]{:S(2)}) copy-start(s32[8008,10]{0,1:T(8,128)} %param.7) | copy-start | bytes 960964
  1.9 1.4 %copy-start.1 = (bf16[2048,336]{1,0:T(8,128)(2,1)S(1)}, bf16[2048,336]{1,0:T(8,128)(2,1)}, u32[]{:S(2)}) copy-start(bf16[2048,336]{1,0:T(8,128)(2,1)} %constant.18.clone.picks_hbm) | copy-start | bytes 4128772
  3.3 0.9 %copy-start.2 = (f32[512,48]{0,1:T(8,128)S(1)}, f32[512,48]{0,1:T(8,128)}, u32[]{:S(2)}) copy-start(f32[512,48]{0,1:T(8,128)} %param.6) | copy-start | bytes 294916
  4.2 0.7 copy-start.3

commit v6 on v5

--- a/solution.py
+++ b/solution.py
@@ -316,6 +316,17 @@
 
         forward(mine_h).start()
         each(1, half, start, 0)
+
+        def along(step):
+            h = wrap(mine_h + half - step, half)
+            return h, 2 * h + mine_p
+
+        def pass_on(step):
+            h, q = along(step)
+            spread(h, q).wait_recv()
+            forward(h).start()
+
+        pass_on(1)
         alpha = jnp.sqrt(told(norm_phase, True) + EPS)
 
         def product(q, acc):
@@ -327,10 +338,8 @@
             )
 
         def hand_on(step, acc):
-            h = wrap(mine_h + half - step, half)
-            spread(h, 2 * h + mine_p).wait_recv()
-            forward(h).start()
-            return product(2 * h + mine_p, acc)
+            pass_on(step)
+            return product(along(step - 1)[1], acc)
 
         def from_pair(step, acc):
             h = wrap(mine_h + half - step, half)
@@ -349,7 +358,8 @@
             return 0
 
         acc = product(me, jnp.zeros((FIELDS, rows), jnp.float32))
-        acc = lax.fori_loop(1, half, hand_on, acc)
+        acc = lax.fori_loop(2, half, hand_on, acc)
+        acc = product(along(half - 1)[1], acc)
         acc = lax.fori_loop(0, half, from_pair, acc)
         cross_out[phase] = acc
         copy = remote(
@@ -438,7 +448,7 @@
             pltpu.VMEM(picks.shape, jnp.bfloat16),
         ],
         compiler_params=pltpu.CompilerParams(
-            collective_id=0, has_side_effects=True, vmem_limit_bytes=44 * 1024 * 1024
+            collective_id=0, has_side_effects=True, vmem_limit_bytes=56 * 1024 * 1024
         ),
     )(points, observed.T, my_terms, jnp.asarray(picks, jnp.bfloat16), jnp.asarray(entries, f32))
     return coeffs.T, left.T

time: 89.3 us -> 90.7 us (1.016)
  Pallas kernels: 82.7 us -> 84.8 us
    pallas_call x1, Pallas kernels: 82.7 us -> 84.8 us  [per_device(): pl.pallas_call(functools.partial(fit_kernel, n, width, share, inverse_roo...]
    unnamed x10 -> x6, local copies, waits for them, and re-layouts: 4.74 us -> 2.75 us
where the time goes in v6:
time: 90.7 us; the launch traced here: 90.5 us
  Pallas kernels  84.8 us (93%)
  local copies, waits for them, and re-layouts  5.04 us (6%)
    pallas_call x1, Pallas kernels, per_device(): pl.pallas_call(functools.partial(fit_kernel, n, width, share, inverse_roo...  84.8 us
    unnamed x6, local copies, waits for them, and re-layouts  2.75 us

profile of v6, /device:TPU:0, one launch (start us, length us, event | category | flops | bytes accessed | tf_op | source)
XLA Modules:
  0.0 90.5 jit_solution(8007615228483181540)
XLA Ops:
  0.6 0.0 copy-start
  0.6 1.4 %pad.8.points_ref = f32[16,512]{1,0:T(8,128)} pad(f32[10,512]{1,0:T(8,128)} %bitcast.9, f32[]{:T(128)} %constant.4.clone.1), padding=0_6x0_0 | pad | bytes 53252 | tf_op jit(solution)/shard_map/jit(_pad)/pad | solution.py:424
  2.1 0.0 copy-done
  2.1 0.1 dynamic-slice_bitcast_fusion
  2.2 0.7 pad.9.index_ref
  2.9 84.8 %shard_map.68 = (f32[48,4004]{1,0:T(8,128)}, f32[48,512]{1,0:T(8,128)}) custom-call(f32[16,512]{1,0:T(8,128)} %pad.8.points_ref, f32[48,512]{1,0:T(8,128)} %bitcast.8, s32[16,4096]{1,0:T(8,128)} %pad.9.index_ref, bf16[2048,336]{1,0:T(8,128)(2,1)} %constant.18.clone.picks_hbm, f32[8,256]{1,0:T(8,128)} %constant.19.clone.entries_ref), custom_call_target="tpu_custom_call" | custom-call | tf_op jit(solution)/shard_map/pallas_call | solution.py:429
  87.7 0.0 copy-start.1
  87.8 2.1 %copy.9 = f32[4004,48]{0,1:T(8,128)} copy(f32[4004,48]{0,1:T(8,128)} %bitcast.6) | data formatting | bytes 1537536
  89.8 0.0 copy-done.1
  89.9 0.6 copy.10
Async XLA Ops:
  0.6 1.5 %copy-start = (s32[8008,10]{0,1:T(8,128)S(1)}, s32[8008,10]{0,1:T(8,128)}, u32[]{:S(2)}) copy-start(s32[8008,10]{0,1:T(8,128)} %param.7) | copy-start | bytes 960964
  87.7 2.1 %copy-start.1 = (f32[48,512]{1,0:T(8,128)S(1)}, f32[48,512]{1,0:T(8,128)}, u32[]{:S(2)}) copy-start(f32[48,512]{1,0:T(8,128)} %get-tuple-element.5) | copy-start | bytes 294916
